TPU v7x, 512 devices: a whole 4x8x8 slice. The times are simulated.
512 devices in a mesh: section: 8 (over x, core), dp: 64 (over y, z).
Axes of the slice: x: 4, y: 8, z: 8, core: 2. Of those that a mesh axis runs over, the one named last changes fastest.
Arguments:
- hidden_in: bfloat16 [64, 192, 1024], P('dp'), may hold values from -6 to 6
- cotangent: bfloat16 [64, 192, 1024], P('dp'), may hold values from -0.15625 to 0.15625
- segments: int32 [64, 192], P('dp'), may hold values from 0 to 23, never falling along the last dimension, each value on 1 to 48 neighbouring positions
- attn_weights: bfloat16 [8, 3, 1024, 1024], P('section', None, 'dp'), may hold values from -8 to 8
- out_weight: bfloat16 [8, 1024, 1024], P('section', 'dp'), may hold values from -0.1875 to 0.1875
Outputs:
- grad_out: float32 [8, 1024, 1024], P('section', 'dp')
Inputs may be any that keep to these rules, and one draw needn't show every extreme that they name: `segments`: along each context the ids never fall, each id from 0 to 23 occurs and covers 1 to 48 positions, one of them exactly 48.
All inputs are finite; a program needn't handle non-finite values.
Results may differ from a plain program's by a relative error of at most 0.029.
Values may be sent and summed in bfloat16 or wider, within the bound.
A program may use at most 64 MiB of HBM per device.

v0:
```python
import jax
import jax.numpy as jnp
from jax import lax
from jax.sharding import PartitionSpec as P

HEADS = 16
NCHUNK = 4


epsilon = 1e-05
masked_score = -1e30


def from_behind(value, axis, steps):
    count = lax.axis_size(axis)
    first, last = (max(0, -steps), min(count, count - steps))
    return lax.ppermute(value, axis, [(source, source + steps) for source in range(first, last)])


def normalize(hidden):
    widened = hidden.astype(jnp.float32)
    row_scale = lax.rsqrt(jnp.mean(widened * widened, axis=-1, keepdims=True) + epsilon)
    return (widened * row_scale).astype(jnp.bfloat16)


def project(normed, weight):
    return jnp.einsum("td,ed->te", normed, weight, preferred_element_type=jnp.float32).astype(
        jnp.bfloat16
    )


def attend(queries, key_rows, values, allowed):
    query_count = queries.shape[0]
    key_count = key_rows.shape[0]
    head_size = queries.shape[1] // HEADS
    query_heads = queries.reshape(query_count, HEADS, head_size)
    key_heads = key_rows.reshape(key_count, HEADS, head_size)
    value_heads = values.reshape(key_count, HEADS, head_size)
    scores = jnp.einsum(
        "qhd,khd->hqk", query_heads, key_heads, preferred_element_type=jnp.float32
    ) * head_size ** (-0.5)
    scores = jnp.where(allowed[None], scores, masked_score)
    weights = jax.nn.softmax(scores, axis=-1).astype(jnp.bfloat16)
    mixed_heads = jnp.einsum(
        "hqk,khd->qhd", weights, value_heads, preferred_element_type=jnp.float32
    )
    return mixed_heads.reshape(query_count, HEADS * head_size).astype(jnp.bfloat16)


def block_layer(inputs, key_cache, value_cache, attn_all, out_all, offset, allowed):
    normed = normalize(inputs)
    queries = project(normed, attn_all[0])
    key_new = project(normed, attn_all[1])
    value_new = project(normed, attn_all[2])
    key_rows = lax.dynamic_update_slice_in_dim(key_cache, key_new, offset, 0)
    value_rows = lax.dynamic_update_slice_in_dim(value_cache, value_new, offset, 0)
    mixed_heads = attend(queries, key_rows, value_rows, allowed)
    added = inputs.astype(jnp.float32) + jnp.einsum(
        "td,ed->te", mixed_heads, out_all, preferred_element_type=jnp.float32
    )
    return ((added.astype(jnp.bfloat16), key_new, value_new), mixed_heads)


def local(hidden_in, cotangent, segments, attn_weights, out_weight):
    attn_all, out_all = (
        lax.all_gather(attn_weights[0], "dp", axis=1, tiled=True),
        lax.all_gather(out_weight[0], "dp", axis=0, tiled=True),
    )
    section_index = lax.axis_index("section")
    section_count = lax.axis_size("section")
    context = hidden_in[0]
    context_cot = cotangent[0]
    length = context.shape[0]
    width = context.shape[1]
    block_rows = length // NCHUNK
    positions = jnp.arange(length, dtype=jnp.int32)
    causal = positions[None, :] <= positions[:, None]
    same_segment = segments[0][:, None] == segments[0][None, :]
    allowed_all = causal & (same_segment | (section_index % 2 == 1))
    moments = NCHUNK + section_count - 1

    def forward_step(moment, loop_state):
        outbox, stored, key_cache, value_cache = loop_state
        received = from_behind(outbox, "section", 1)
        block_index = moment - section_index
        is_valid = (block_index >= 0) & (block_index < NCHUNK)
        offset = jnp.clip(block_index, 0, NCHUNK - 1) * block_rows
        from_input = lax.dynamic_slice_in_dim(context, offset, block_rows, 0)
        inputs = jnp.where(section_index == 0, from_input, received)
        allowed = lax.dynamic_slice_in_dim(allowed_all, offset, block_rows, 0)

        def advance(unused):
            results, unused_mixed = block_layer(
                inputs, key_cache, value_cache, attn_all, out_all, offset, allowed
            )
            output, key_new, value_new = results
            return (
                output,
                lax.dynamic_update_slice_in_dim(stored, inputs, offset, 0),
                lax.dynamic_update_slice_in_dim(key_cache, key_new, offset, 0),
                lax.dynamic_update_slice_in_dim(value_cache, value_new, offset, 0),
            )

        def forward_remain(unused):
            return (outbox, stored, key_cache, value_cache)

        return lax.cond(is_valid, advance, forward_remain, 0)

    zeros_block = jnp.zeros((block_rows, width), jnp.bfloat16)
    zeros_full = jnp.zeros_like(context)
    final_state = lax.fori_loop(
        0, moments, forward_step, (zeros_block, zeros_full, zeros_full, zeros_full)
    )
    stored = final_state[1]
    key_cache = final_state[2]
    value_cache = final_state[3]
    zeros_grad = jnp.zeros(context.shape, jnp.float32)
    start_extra = jnp.zeros(out_all.shape, jnp.float32)

    def backward_step(moment, loop_state):
        outbox, key_grad, value_grad, extra = loop_state
        received = from_behind(outbox, "section", -1)
        block_index = NCHUNK - 1 - moment + (section_count - 1 - section_index)
        is_valid = (block_index >= 0) & (block_index < NCHUNK)
        offset = jnp.clip(block_index, 0, NCHUNK - 1) * block_rows
        from_cot = lax.dynamic_slice_in_dim(context_cot, offset, block_rows, 0)
        d_output = jnp.where(section_index == section_count - 1, from_cot, received)
        inputs = lax.dynamic_slice_in_dim(stored, offset, block_rows, 0)
        allowed = lax.dynamic_slice_in_dim(allowed_all, offset, block_rows, 0)

        def retreat(unused):

            def local_layer(inputs_in, keys_in, values_in):
                return block_layer(
                    inputs_in, keys_in, values_in, attn_all, out_all, offset, allowed
                )

            unused_out, pullback, mixed_heads = jax.vjp(
                local_layer, inputs, key_cache, value_cache, has_aux=True
            )
            own_keys = lax.dynamic_slice_in_dim(key_grad, offset, block_rows, 0).astype(
                jnp.bfloat16
            )
            own_values = lax.dynamic_slice_in_dim(value_grad, offset, block_rows, 0).astype(
                jnp.bfloat16
            )
            d_inputs, d_keys, d_values = pullback((d_output, own_keys, own_values))
            new_extra = extra + jnp.einsum(
                "te,td->ed", d_output, mixed_heads, preferred_element_type=jnp.float32
            )
            return (d_inputs, d_keys.astype(jnp.float32), d_values.astype(jnp.float32), new_extra)

        def backward_remain(unused):
            return (outbox, zeros_grad, zeros_grad, extra)

        d_inputs, d_keys, d_values, extra = lax.cond(is_valid, retreat, backward_remain, 0)
        return (d_inputs, key_grad + d_keys, value_grad + d_values, extra)

    back_state = lax.fori_loop(
        0, moments, backward_step, (zeros_block, zeros_grad, zeros_grad, start_extra)
    )
    rounded = lax.optimization_barrier(back_state[3].astype(jnp.bfloat16))
    result = lax.psum_scatter(rounded.astype(jnp.float32), "dp", scatter_dimension=0, tiled=True)
    return result[None]


def solution(mesh):
    in_specs = (
        P("dp", None, None),
        P("dp", None, None),
        P("dp", None),
        P("section", None, "dp", None),
        P("section", "dp", None),
    )
    out_specs = P("section", "dp", None)
    return jax.shard_map(local, mesh=mesh, in_specs=in_specs, out_specs=out_specs, check_vma=False)
```

profile of v0, /device:TPU:1, one launch (start us, length us, event | category | flops | bytes accessed | tf_op | source)
XLA Modules:
  0.0 1707.2 jit_solution(352044906562151435)
XLA Ops:
  8.1 87.6 %all-gather.5.cloned.1.call-done = bf16[1,1024,1024]{2,1,0:T(8,128)(2,1)} async-done(((bf16[1,16,1024]{2,1,0:T(8,128)(2,1)}), bf16[1,1024,1024]{2,1,0:T(8,128)(2,1)}) %all-gather.5.cloned.1.call-update) | async-done | bytes 2097168 | tf_op jit(solution)/shard_map/all_gather | solution.py:67
  95.7 93.9 %all-gather.7.cloned.1.call-done = bf16[1,3,1024,1024]{3,2,1,0:T(8,128)(2,1)} async-done(((bf16[1,3,16,1024]{3,2,1,0:T(8,128)(2,1)}), bf16[1,3,1024,1024]{3,2,1,0:T(8,128)(2,1)}) %all-gather.7.cloned.1.call-update) | async-done | bytes 6291472 | tf_op jit(solution)/shard_map/all_gather | solution.py:66
  192.8 252.2 %while.43 = (s32[]{:T(128)}, bf16[48,1024]{1,0:T(8,128)(2,1)}, bf16[192,1024]{1,0:T(8,128)(2,1)}, bf16[192,1024]{0,1:T(8,128)(2,1)}, bf16[192,1024]{0,1:T(8,128)...) while((s32[]{:T(128)}, bf16[48,1024]{1,0:T(8,128)(2,1)}, ...), condition=%wide.region_6.7_spmd.clone, body=%wide.region_0.6_spmd.clone.sunk | while | flops 461624512 | bytes 22983124 | solution.py:111
  192.8 4.3 collective-permute-start
  199.1 4.2 collective-permute-start
  203.4 20.2 %collective-permute-done = bf16[48,1024]{1,0:T(8,128)(2,1)S(1)} collective-permute-done((bf16[48,1024]{1,0:T(8,128)(2,1)}, bf16[48,1024]{1,0:T(8,128)(2,1)S(1)}, u32[]{:S(2)}, u32[]{:S(2)}) %collective-permute-start) | collective-permute-done | bytes 98336 | tf_op jit(solution)/shard_map/while/body/eval_jaxpr/ppermute | solution.py:17
  223.6 24.7 %conditional.6 = ((bf16[48,1024]{1,0:T(8,128)(2,1)}, bf16[192,1024]{1,0:T(8,128)(2,1)}, bf16[192,1024]{0,1:T(8,128)(2,1)}, bf16[192,1024]{0,1:T(8,128)(2,1)})) conditional(s32[]{:T(128)} %convert_element_type.351, (bf16[48,1024]{1,0:T(8,128)(2,1)}, bf16[192,1024]{1,0:T(8,128)(2,1)}, bf16[192,1024]{0,1:T(8,128)(2,1)}, ...), branch_computations={%region_1.1_spmd, %region_2.5_spmd} | conditional | flops 461624512 | bytes 22294624 | solution.py:107
  252.2 25.6 %conditional.6 = ((bf16[48,1024]{1,0:T(8,128)(2,1)}, bf16[192,1024]{1,0:T(8,128)(2,1)}, bf16[192,1024]{0,1:T(8,128)(2,1)}, bf16[192,1024]{0,1:T(8,128)(2,1)})) conditional(s32[]{:T(128)} %convert_element_type.351, (bf16[48,1024]{1,0:T(8,128)(2,1)}, bf16[192,1024]{1,0:T(8,128)(2,1)}, bf16[192,1024]{0,1:T(8,128)(2,1)}, ...), branch_computations={%region_1.1_spmd, %region_2.5_spmd} | conditional | flops 461624512 | bytes 22294624 | solution.py:107
  263.1 3.9 dynamic_update_slice.45
  268.6 3.9 dynamic_update_slice.44
  283.1 25.5 %conditional.6 = ((bf16[48,1024]{1,0:T(8,128)(2,1)}, bf16[192,1024]{1,0:T(8,128)(2,1)}, bf16[192,1024]{0,1:T(8,128)(2,1)}, bf16[192,1024]{0,1:T(8,128)(2,1)})) conditional(s32[]{:T(128)} %convert_element_type.351, (bf16[48,1024]{1,0:T(8,128)(2,1)}, bf16[192,1024]{1,0:T(8,128)(2,1)}, bf16[192,1024]{0,1:T(8,128)(2,1)}, ...), branch_computations={%region_1.1_spmd, %region_2.5_spmd} | conditional | flops 461624512 | bytes 22294624 | solution.py:107
  294.0 3.9 dynamic_update_slice.45
  299.5 3.9 dynamic_update_slice.44
  308.7 4.2 collective-permute-start
  314.9 24.3 %conditional.6 = ((bf16[48,1024]{1,0:T(8,128)(2,1)}, bf16[192,1024]{1,0:T(8,128)(2,1)}, bf16[192,1024]{0,1:T(8,128)(2,1)}, bf16[192,1024]{0,1:T(8,128)(2,1)})) conditional(s32[]{:T(128)} %convert_element_type.351, (bf16[48,1024]{1,0:T(8,128)(2,1)}, bf16[192,1024]{1,0:T(8,128)(2,1)}, bf16[192,1024]{0,1:T(8,128)(2,1)}, ...), branch_computations={%region_1.1_spmd, %region_2.5_spmd} | conditional | flops 461624512 | bytes 22294624 | solution.py:107
  339.2 5.4 collective-permute-start
  346.6 28.5 %collective-permute-start = (bf16[48,1024]{1,0:T(8,128)(2,1)}, bf16[48,1024]{1,0:T(8,128)(2,1)S(1)}, u32[]{:S(2)}, u32[]{:S(2)}) collective-permute-start(bf16[48,1024]{1,0:T(8,128)(2,1)} %get-tuple-element.1357), channel_id=1, source_target_pairs={{0,64},{64,128},{128,192},{192,256},{256,320},{320,384},{384,448},... | collective-permute-start | bytes 294920 | tf_op jit(solution)/shard_map/while/body/eval_jaxpr/ppermute | solution.py:17
  377.1 4.2 collective-permute-start
  383.4 22.7 %collective-permute-start = (bf16[48,1024]{1,0:T(8,128)(2,1)}, bf16[48,1024]{1,0:T(8,128)(2,1)S(1)}, u32[]{:S(2)}, u32[]{:S(2)}) collective-permute-start(bf16[48,1024]{1,0:T(8,128)(2,1)} %get-tuple-element.1357), channel_id=1, source_target_pairs={{0,64},{64,128},{128,192},{192,256},{256,320},{320,384},{384,448},... | collective-permute-start | bytes 294920 | tf_op jit(solution)/shard_map/while/body/eval_jaxpr/ppermute | solution.py:17
  408.0 4.4 collective-permute-start
  414.4 28.5 %collective-permute-start = (bf16[48,1024]{1,0:T(8,128)(2,1)}, bf16[48,1024]{1,0:T(8,128)(2,1)S(1)}, u32[]{:S(2)}, u32[]{:S(2)}) collective-permute-start(bf16[48,1024]{1,0:T(8,128)(2,1)} %get-tuple-element.1357), channel_id=1, source_target_pairs={{0,64},{64,128},{128,192},{192,256},{256,320},{320,384},{384,448},... | collective-permute-start | bytes 294920 | tf_op jit(solution)/shard_map/while/body/eval_jaxpr/ppermute | solution.py:17
  447.5 943.0 %while.44 = (s32[]{:T(128)}, bf16[48,1024]{1,0:T(8,128)(2,1)S(1)}, f32[192,1024]{0,1:T(8,128)}, f32[192,1024]{0,1:T(8,128)}, f32[1024,1024]{1,0:T(8,128)}, /*ind...) while((s32[]{:T(128)}, bf16[48,1024]{1,0:T(8,128)(2,1)S(1)}, ...), condition=%wide.region_15.16_spmd.clone, body=%wide.region_7.15_spmd.clone.sunk | while | flops 1004234432 | bytes 83600648 | solution.py:159
  467.2 19.6 %collective-permute-done.1 = bf16[48,1024]{1,0:T(8,128)(2,1)S(1)} collective-permute-done((bf16[48,1024]{1,0:T(8,128)(2,1)S(1)}, bf16[48,1024]{1,0:T(8,128)(2,1)S(1)}, u32[]{:S(2)}, u32[]{:S(2)}) %collective-permute-start.1) | collective-permute-done | bytes 98336 | tf_op jit(solution)/shard_map/while/body/eval_jaxpr/ppermute | solution.py:17
  515.3 25.5 %collective-permute-done.1 = bf16[48,1024]{1,0:T(8,128)(2,1)S(1)} collective-permute-done((bf16[48,1024]{1,0:T(8,128)(2,1)S(1)}, bf16[48,1024]{1,0:T(8,128)(2,1)S(1)}, u32[]{:S(2)}, u32[]{:S(2)}) %collective-permute-start.1) | collective-permute-done | bytes 98336 | tf_op jit(solution)/shard_map/while/body/eval_jaxpr/ppermute | solution.py:17
  569.0 19.0 %collective-permute-done.1 = bf16[48,1024]{1,0:T(8,128)(2,1)S(1)} collective-permute-done((bf16[48,1024]{1,0:T(8,128)(2,1)S(1)}, bf16[48,1024]{1,0:T(8,128)(2,1)S(1)}, u32[]{:S(2)}, u32[]{:S(2)}) %collective-permute-start.1) | collective-permute-done | bytes 98336 | tf_op jit(solution)/shard_map/while/body/eval_jaxpr/ppermute | solution.py:17
  601.2 419.8 %collective-permute-done.1 = bf16[48,1024]{1,0:T(8,128)(2,1)S(1)} collective-permute-done((bf16[48,1024]{1,0:T(8,128)(2,1)S(1)}, bf16[48,1024]{1,0:T(8,128)(2,1)S(1)}, u32[]{:S(2)}, u32[]{:S(2)}) %collective-permute-start.1) | collective-permute-done | bytes 98336 | tf_op jit(solution)/shard_map/while/body/eval_jaxpr/ppermute | solution.py:17
  1022.4 72.5 %conditional.7 = (bf16[48,1024]{1,0:T(8,128)(2,1)S(1)}, f32[192,1024]{0,1:T(8,128)}, f32[192,1024]{0,1:T(8,128)}, f32[1024,1024]{1,0:T(8,128)}) conditional(s32[]{:T(128)} %convert_element_type.352, (bf16[48,1024]{1,0:T(8,128)(2,1)S(1)}, f32[1024,1024]{1,0:T(8,128)}) %tuple.136, (pred[]{:T(512)}, s32[]{:T(128)}, bf16[192,1024]{1,0:T(8,128)(2,1)}, ...), branch_computations={%region_8.8_spmd, %region_9.14_spmd} | conditional | flops 1003448000 | bytes 75047768 | solution.py:156
  1059.3 3.8 fusion.65
  1063.1 3.9 convolution_convert_fusion.1
  1104.5 16.2 collective-permute-done.1
  1122.1 75.3 %conditional.7 = (bf16[48,1024]{1,0:T(8,128)(2,1)S(1)}, f32[192,1024]{0,1:T(8,128)}, f32[192,1024]{0,1:T(8,128)}, f32[1024,1024]{1,0:T(8,128)}) conditional(s32[]{:T(128)} %convert_element_type.352, (bf16[48,1024]{1,0:T(8,128)(2,1)S(1)}, f32[1024,1024]{1,0:T(8,128)}) %tuple.136, (pred[]{:T(512)}, s32[]{:T(128)}, bf16[192,1024]{1,0:T(8,128)(2,1)}, ...), branch_computations={%region_8.8_spmd, %region_9.14_spmd} | conditional | flops 1003448000 | bytes 75047768 | solution.py:156
  1140.4 4.0 dynamic_update_slice.47
  1146.2 3.8 dynamic_update_slice.48
  1160.2 3.8 fusion.65
  1164.0 3.9 convolution_convert_fusion.1
  1177.4 3.8 dynamic_update_slice.50
  1181.2 3.9 dynamic_update_slice.49
  1209.7 75.3 %conditional.7 = (bf16[48,1024]{1,0:T(8,128)(2,1)S(1)}, f32[192,1024]{0,1:T(8,128)}, f32[192,1024]{0,1:T(8,128)}, f32[1024,1024]{1,0:T(8,128)}) conditional(s32[]{:T(128)} %convert_element_type.352, (bf16[48,1024]{1,0:T(8,128)(2,1)S(1)}, f32[1024,1024]{1,0:T(8,128)}) %tuple.136, (pred[]{:T(512)}, s32[]{:T(128)}, bf16[192,1024]{1,0:T(8,128)(2,1)}, ...), branch_computations={%region_8.8_spmd, %region_9.14_spmd} | conditional | flops 1003448000 | bytes 75047768 | solution.py:156
  1228.1 4.0 dynamic_update_slice.47
  1233.9 3.8 dynamic_update_slice.48
  1247.8 3.8 fusion.65
  1251.6 3.9 convolution_convert_fusion.1
  1265.0 3.8 dynamic_update_slice.50
  1268.8 3.9 dynamic_update_slice.49
  1297.3 73.6 %conditional.7 = (bf16[48,1024]{1,0:T(8,128)(2,1)S(1)}, f32[192,1024]{0,1:T(8,128)}, f32[192,1024]{0,1:T(8,128)}, f32[1024,1024]{1,0:T(8,128)}) conditional(s32[]{:T(128)} %convert_element_type.352, (bf16[48,1024]{1,0:T(8,128)(2,1)S(1)}, f32[1024,1024]{1,0:T(8,128)}) %tuple.136, (pred[]{:T(512)}, s32[]{:T(128)}, bf16[192,1024]{1,0:T(8,128)(2,1)}, ...), branch_computations={%region_8.8_spmd, %region_9.14_spmd} | conditional | flops 1003448000 | bytes 75047768 | solution.py:156
  1334.6 3.8 fusion.65
  1338.4 3.9 convolution_convert_fusion.1
  1395.5 305.2 %reduce-scatter.2.cloned.1.call-done = f32[16,1024]{1,0:T(8,128)} async-done(((f32[1024,1024]{1,0:T(8,128)}), f32[16,1024]{1,0:T(8,128)}) %reduce-scatter.2.cloned.1.call-update) | async-done | bytes 65552 | tf_op jit(solution)/shard_map/reduce_scatter | solution.py:163
  (410 shorter events, 516.8 us)
Async XLA Ops:
  6.5 89.2 %all-gather.5.cloned.1.call-start = ((), (), s32[]{:S(2)}) async-start(), calls=%async_computation.2 | async-start | bytes 2129920 | tf_op jit(solution)/shard_map/all_gather | solution.py:67
  7.3 182.4 %all-gather.7.cloned.1.call-start = ((), (), s32[]{:S(2)}) async-start(), calls=%async_computation.3 | async-start | bytes 6389760 | tf_op jit(solution)/shard_map/all_gather | solution.py:66
  8.0 1692.7 %reduce-scatter.2.cloned.1.call-start = ((), (), s32[]{:S(2)}) async-start(), calls=%async_computation.1 | async-start | bytes 4259840 | tf_op jit(solution)/shard_map/reduce_scatter | solution.py:163
  192.8 6.3 collective-permute-start
  199.1 24.5 %collective-permute-start = (bf16[48,1024]{1,0:T(8,128)(2,1)}, bf16[48,1024]{1,0:T(8,128)(2,1)S(1)}, u32[]{:S(2)}, u32[]{:S(2)}) collective-permute-start(bf16[48,1024]{1,0:T(8,128)(2,1)} %get-tuple-element.1357), channel_id=1, source_target_pairs={{0,64},{64,128},{128,192},{192,256},{256,320},{320,384},{384,448},... | collective-permute-start | bytes 294920 | tf_op jit(solution)/shard_map/while/body/eval_jaxpr/ppermute | solution.py:17
  237.9 9.0 copy-start
  248.4 3.8 collective-permute-start
  267.0 9.5 copy-start
  277.8 5.3 collective-permute-start
  297.8 9.5 copy-start
  308.7 6.1 collective-permute-start
  329.0 8.8 copy-start
  339.2 7.4 collective-permute-start
  346.6 30.4 %collective-permute-start = (bf16[48,1024]{1,0:T(8,128)(2,1)}, bf16[48,1024]{1,0:T(8,128)(2,1)S(1)}, u32[]{:S(2)}, u32[]{:S(2)}) collective-permute-start(bf16[48,1024]{1,0:T(8,128)(2,1)} %get-tuple-element.1357), channel_id=1, source_target_pairs={{0,64},{64,128},{128,192},{192,256},{256,320},{320,384},{384,448},... | collective-permute-start | bytes 294920 | tf_op jit(solution)/shard_map/while/body/eval_jaxpr/ppermute | solution.py:17
  377.1 6.1 collective-permute-start
  383.4 24.6 %collective-permute-start = (bf16[48,1024]{1,0:T(8,128)(2,1)}, bf16[48,1024]{1,0:T(8,128)(2,1)S(1)}, u32[]{:S(2)}, u32[]{:S(2)}) collective-permute-start(bf16[48,1024]{1,0:T(8,128)(2,1)} %get-tuple-element.1357), channel_id=1, source_target_pairs={{0,64},{64,128},{128,192},{192,256},{256,320},{320,384},{384,448},... | collective-permute-start | bytes 294920 | tf_op jit(solution)/shard_map/while/body/eval_jaxpr/ppermute | solution.py:17
  408.0 6.3 collective-permute-start
  414.4 30.4 %collective-permute-start = (bf16[48,1024]{1,0:T(8,128)(2,1)}, bf16[48,1024]{1,0:T(8,128)(2,1)S(1)}, u32[]{:S(2)}, u32[]{:S(2)}) collective-permute-start(bf16[48,1024]{1,0:T(8,128)(2,1)} %get-tuple-element.1357), channel_id=1, source_target_pairs={{0,64},{64,128},{128,192},{192,256},{256,320},{320,384},{384,448},... | collective-permute-start | bytes 294920 | tf_op jit(solution)/shard_map/while/body/eval_jaxpr/ppermute | solution.py:17
  444.9 2.6 copy-start.1
  444.9 2.6 copy-start.6
  447.5 6.5 collective-permute-start.1
  462.6 24.2 %collective-permute-start.1 = (bf16[48,1024]{1,0:T(8,128)(2,1)S(1)}, bf16[48,1024]{1,0:T(8,128)(2,1)S(1)}, u32[]{:S(2)}, u32[]{:S(2)}) collective-permute-start(bf16[48,1024]{1,0:T(8,128)(2,1)S(1)} %get-tuple-element.1406), channel_id=1, source_target_pairs={{64,0},{128,64},{192,128},{256,192},{320,256},{384,320},{448,384},... | collective-permute-start | bytes 294920 | tf_op jit(solution)/shard_map/while/body/eval_jaxpr/ppermute | solution.py:17
  495.4 6.7 collective-permute-start.1
  510.7 30.1 %collective-permute-start.1 = (bf16[48,1024]{1,0:T(8,128)(2,1)S(1)}, bf16[48,1024]{1,0:T(8,128)(2,1)S(1)}, u32[]{:S(2)}, u32[]{:S(2)}) collective-permute-start(bf16[48,1024]{1,0:T(8,128)(2,1)S(1)} %get-tuple-element.1406), channel_id=1, source_target_pairs={{64,0},{128,64},{192,128},{256,192},{320,256},{384,320},{448,384},... | collective-permute-start | bytes 294920 | tf_op jit(solution)/shard_map/while/body/eval_jaxpr/ppermute | solution.py:17
  549.3 6.5 collective-permute-start.1
  564.4 23.6 %collective-permute-start.1 = (bf16[48,1024]{1,0:T(8,128)(2,1)S(1)}, bf16[48,1024]{1,0:T(8,128)(2,1)S(1)}, u32[]{:S(2)}, u32[]{:S(2)}) collective-permute-start(bf16[48,1024]{1,0:T(8,128)(2,1)S(1)} %get-tuple-element.1406), channel_id=1, source_target_pairs={{64,0},{128,64},{192,128},{256,192},{320,256},{384,320},{448,384},... | collective-permute-start | bytes 294920 | tf_op jit(solution)/shard_map/while/body/eval_jaxpr/ppermute | solution.py:17
  596.6 424.4 %collective-permute-start.1 = (bf16[48,1024]{1,0:T(8,128)(2,1)S(1)}, bf16[48,1024]{1,0:T(8,128)(2,1)S(1)}, u32[]{:S(2)}, u32[]{:S(2)}) collective-permute-start(bf16[48,1024]{1,0:T(8,128)(2,1)S(1)} %get-tuple-element.1406), channel_id=1, source_target_pairs={{64,0},{128,64},{192,128},{256,192},{320,256},{384,320},{448,384},... | collective-permute-start | bytes 294920 | tf_op jit(solution)/shard_map/while/body/eval_jaxpr/ppermute | solution.py:17
  1059.3 7.8 copy-start.4
  1084.4 7.6 copy-start.2
  1084.4 7.6 copy-start.5
  1092.8 2.0 copy-start.3
  1099.9 20.8 %collective-permute-start.1 = (bf16[48,1024]{1,0:T(8,128)(2,1)S(1)}, bf16[48,1024]{1,0:T(8,128)(2,1)S(1)}, u32[]{:S(2)}, u32[]{:S(2)}) collective-permute-start(bf16[48,1024]{1,0:T(8,128)(2,1)S(1)} %get-tuple-element.1406), channel_id=1, source_target_pairs={{64,0},{128,64},{192,128},{256,192},{320,256},{384,320},{448,384},... | collective-permute-start | bytes 294920 | tf_op jit(solution)/shard_map/while/body/eval_jaxpr/ppermute | solution.py:17
  1160.2 7.8 copy-start.4
  1186.8 7.6 copy-start.2
  1186.8 7.6 copy-start.5
  1195.3 2.0 copy-start.3
  1202.4 5.9 collective-permute-start.1
  1247.8 7.8 copy-start.4
  1274.5 7.6 copy-start.2
  1274.5 7.6 copy-start.5
  1282.9 2.0 copy-start.3
  1290.0 5.9 collective-permute-start.1
  1334.6 7.8 copy-start.4
  1360.4 7.6 copy-start.2
  1360.4 7.6 copy-start.5
  1368.9 2.0 copy-start.3
  1376.0 5.9 collective-permute-start.1
Sparse Core Ops, SparseCore 0:
  10.4 85.2 all-gather.4
  98.8 90.8 all-gather.6
  1395.6 305.0 reduce-scatter.1
where the time goes:
time: 1720 us; the launch traced here: 1710 us
  waiting for transfers between devices  1040 us (60%)
  matrix products  205 us (12%)
  local copies, waits for them, and re-layouts  185 us (11%)
  starting transfers between devices  133 us (8%)
  other arithmetic  131 us (8%)
    ppermute x22, waiting for transfers between devices, from_behind(): lax.ppermute(value, axis, [(source, source + steps) for source in range(f...  551 us
    reduce_scatter x1, waiting for transfers between devices, local(): lax.psum_scatter(rounded.astype(jnp.float32), 'dp', scatter_dimension=0,...  305 us
    ppermute x22, starting transfers between devices, from_behind(): lax.ppermute(value, axis, [(source, source + steps) for source in range(f...  133 us
    dot_general x36, matrix products, project(): jnp.einsum('td,ed->te', normed, weight, preferred_element_type=jnp.float32)  94.6 us
    all_gather x1, waiting for transfers between devices, local(): lax.all_gather(attn_weights[0], 'dp', axis=1, tiled=True)  93.9 us
    all_gather x1, waiting for transfers between devices, local(): lax.all_gather(out_weight[0], 'dp', axis=0, tiled=True)  87.6 us
    add x22, other arithmetic, backward_step(): return (d_inputs, key_grad + d_keys, value_grad + d_values, extra)  55.6 us
    dot_general x16, matrix products, attend(): jnp.einsum('hqk,khd->qhd', weights, value_heads, preferred_element_type=j...  47.3 us
  transfers between devices with their start and end apart: 25, of which 25 were waited for; matrix products, arithmetic and copies ran while one was open for 2% of the time, Pallas kernels for 0%

commit v1 on v0

v1 whole, which is shorter than its diff:
```python
import functools
import jax
import jax.numpy as jnp
from jax import lax
from jax.experimental import pallas as pl
from jax.experimental.pallas import tpu as pltpu
from jax.sharding import PartitionSpec as P

MESH = pl.DeviceIdType.MESH
HEADS = 16
HEAD_DIM = 64
PAIRS = HEADS // 2
PAIR = 2 * HEAD_DIM
NC = 2
SECTIONS = 8
epsilon = 1e-05
masked_score = -1e30

NT = (((1,), (1,)), ((), ()))
NN = (((1,), (0,)), ((), ()))
TN = (((0,), (0,)), ((), ()))


def dot(a, b, dims):
    return lax.dot_general(a, b, dims, preferred_element_type=jnp.float32)


def halves(block, low):
    zero = jnp.zeros_like(block)
    return jnp.concatenate([jnp.where(low, block, zero), jnp.where(low, zero, block)], axis=0)


def pipeline_kernel(
    x_ref, cot_ref, bias_ref, w_ref, dw_ref,
    hid, outb, gin, gout, qb, kb, vb, mixb, pb, dmb, dqb, dkb, dvb,
    fsend, frecv, bsend, brecv,
):
    s = lax.axis_index("section")
    length, width = x_ref.shape
    rows_c = length // NC
    barrier = pltpu.get_barrier_semaphore()

    for step in (1, SECTIONS - 1):
        other = lax.rem(s + step, SECTIONS)
        pl.semaphore_signal(barrier, inc=1, device_id={"section": other}, device_id_type=MESH)
    pl.semaphore_wait(barrier, 2)

    def forward_copy(c):
        rows = pl.ds(c * rows_c, rows_c)
        return pltpu.make_async_remote_copy(
            src_ref=outb.at[rows], dst_ref=hid.at[rows], send_sem=fsend.at[c], recv_sem=frecv.at[c],
            device_id={"section": jnp.minimum(s + 1, SECTIONS - 1)}, device_id_type=MESH,
        )

    def backward_copy(c):
        rows = pl.ds(c * rows_c, rows_c)
        return pltpu.make_async_remote_copy(
            src_ref=gout.at[rows], dst_ref=gin.at[rows], send_sem=bsend.at[c], recv_sem=brecv.at[c],
            device_id={"section": jnp.maximum(s - 1, 0)}, device_id_type=MESH,
        )

    @pl.when(s == 0)
    def _():
        hid[...] = x_ref[...]

    @pl.when(s == SECTIONS - 1)
    def _():
        gin[...] = cot_ref[...]

    dkb[...] = jnp.zeros_like(dkb)
    dvb[...] = jnp.zeros_like(dvb)
    low = lax.broadcasted_iota(jnp.int32, (rows_c, PAIR), 1) < HEAD_DIM

    for c in range(NC):
        lo, hi = c * rows_c, (c + 1) * rows_c

        @pl.when(s > 0)
        def _():
            forward_copy(c).wait_recv()

        h = hid[lo:hi].astype(jnp.float32)
        r = lax.rsqrt(jnp.mean(h * h, axis=-1, keepdims=True) + epsilon)
        normed = (h * r).astype(jnp.bfloat16)
        for j, buf in ((0, qb), (1, kb), (2, vb)):
            buf[lo:hi] = dot(normed, w_ref[j], NT).astype(jnp.bfloat16)
        bias = bias_ref[lo:hi, :hi]
        bias2 = jnp.concatenate([bias, bias], axis=0)
        for p in range(PAIRS):
            cols = slice(p * PAIR, (p + 1) * PAIR)
            q01 = halves(qb[lo:hi, cols], low)
            scores = dot(q01, kb[:hi, cols], NT) * HEAD_DIM ** (-0.5) + bias2
            top = jnp.max(scores, axis=-1, keepdims=True)
            e = jnp.exp(scores - top)
            weights = (e / jnp.sum(e, axis=-1, keepdims=True)).astype(jnp.bfloat16)
            pb[c, p, :, :hi] = weights
            o = dot(weights, vb[:hi, cols], NN)
            mixb[lo:hi, cols] = jnp.where(low, o[:rows_c], o[rows_c:]).astype(jnp.bfloat16)

        @pl.when(s < SECTIONS - 1)
        def _():
            added = hid[lo:hi].astype(jnp.float32) + dot(mixb[lo:hi], w_ref[3], NT)
            outb[lo:hi] = added.astype(jnp.bfloat16)
            forward_copy(c).start()

    for c in reversed(range(NC)):
        lo, hi = c * rows_c, (c + 1) * rows_c

        @pl.when(s < SECTIONS - 1)
        def _():
            backward_copy(c).wait_recv()

        @pl.when(s > 0)
        def _():
            g = gin[lo:hi]
            dmb[...] = dot(g, w_ref[3], NN).astype(jnp.bfloat16)
            for p in range(PAIRS):
                cols = slice(p * PAIR, (p + 1) * PAIR)
                d01 = halves(dmb[:, cols], low)
                q01 = halves(qb[lo:hi, cols], low)
                weights = pb[c, p, :, :hi]
                wide = weights.astype(jnp.float32)
                dweights = dot(d01, vb[:hi, cols], NT)
                delta = jnp.sum(wide * dweights, axis=-1, keepdims=True)
                ds = (wide * (dweights - delta) * HEAD_DIM ** (-0.5)).astype(jnp.bfloat16)
                dq01 = dot(ds, kb[:hi, cols], NN)
                dqb[:, cols] = jnp.where(low, dq01[:rows_c], dq01[rows_c:]).astype(jnp.bfloat16)
                dkb[:hi, cols] += dot(ds, q01, TN)
                dvb[:hi, cols] += dot(weights, d01, TN)
            dn = dot(dqb[...], w_ref[0], NN)
            dn += dot(dkb[lo:hi].astype(jnp.bfloat16), w_ref[1], NN)
            dn += dot(dvb[lo:hi].astype(jnp.bfloat16), w_ref[2], NN)
            h = hid[lo:hi].astype(jnp.float32)
            r = lax.rsqrt(jnp.mean(h * h, axis=-1, keepdims=True) + epsilon)
            along = jnp.mean(dn * h, axis=-1, keepdims=True)
            dh = dn * r - h * (r * r * r * along)
            gout[lo:hi] = (g.astype(jnp.float32) + dh).astype(jnp.bfloat16)
            backward_copy(c).start()

    step = 256
    for j in range(0, width, step):
        dw_ref[j : j + step] = dot(gin[:, j : j + step], mixb[...], TN).astype(jnp.bfloat16)

    for c in range(NC):
        @pl.when(s < SECTIONS - 1)
        def _():
            forward_copy(c).wait_send()

        @pl.when(s > 0)
        def _():
            backward_copy(c).wait_send()


def pipeline(context, cot, bias, weights):
    length, width = context.shape
    rows_c = length // NC
    full = pltpu.VMEM((length, width), jnp.bfloat16)
    return pl.pallas_call(
        pipeline_kernel,
        name="pipeline",
        out_shape=jax.ShapeDtypeStruct((width, width), jnp.bfloat16),
        in_specs=[pl.BlockSpec(memory_space=pltpu.VMEM)] * 4,
        out_specs=pl.BlockSpec(memory_space=pltpu.VMEM),
        scratch_shapes=[full] * 8 + [
            pltpu.VMEM((NC, PAIRS, 2 * rows_c, length), jnp.bfloat16),
            pltpu.VMEM((rows_c, width), jnp.bfloat16),
            pltpu.VMEM((rows_c, width), jnp.bfloat16),
            pltpu.VMEM((length, width), jnp.float32),
            pltpu.VMEM((length, width), jnp.float32),
        ] + [pltpu.SemaphoreType.DMA((NC,))] * 4,
        compiler_params=pltpu.CompilerParams(
            collective_id=1, has_side_effects=True, vmem_limit_bytes=48 << 20
        ),
    )(context, cot, bias, weights)


def local(hidden_in, cotangent, segments, attn_weights, out_weight):
    width = out_weight.shape[-1]
    section_index = lax.axis_index("section")
    shard = jnp.concatenate([attn_weights[0], out_weight], axis=0)
    weights = lax.all_gather(shard, "dp", axis=1, tiled=True)
    context = hidden_in[0]
    length = context.shape[0]
    positions = jnp.arange(length, dtype=jnp.int32)
    causal = positions[None, :] <= positions[:, None]
    same_segment = segments[0][:, None] == segments[0][None, :]
    allowed = causal & (same_segment | (section_index % 2 == 1))
    bias = jnp.where(allowed, 0.0, masked_score).astype(jnp.float32)
    grad = pipeline(context, cotangent[0], bias, weights)
    result = lax.psum_scatter(grad.astype(jnp.float32), "dp", scatter_dimension=0, tiled=True)
    return result[None]


def solution(mesh):
    in_specs = (
        P("dp", None, None),
        P("dp", None, None),
        P("dp", None),
        P("section", None, "dp", None),
        P("section", "dp", None),
    )
    return jax.shard_map(
        local, mesh=mesh, in_specs=in_specs, out_specs=P("section", "dp", None), check_vma=False
    )
```

time: 1720 us -> 480 us (0.28)
  waiting for transfers between devices: 1040 us -> 345 us
  matrix products: 205 us -> 0 us
  local copies, waits for them, and re-layouts: 185 us -> 1.99 us
  starting transfers between devices: 133 us -> 0.04 us
  other arithmetic: 131 us -> 4.81 us
  Pallas kernels: 0 us -> 111 us
    ppermute x22 -> x0, waiting for transfers between devices: 551 us -> none  [from_behind(): lax.ppermute(value, axis, [(source, source + steps) for source in range(f...]
    dot_general x76 -> x0, matrix products: 189 us -> none  [the longest x36 94.6 us: project(): jnp.einsum('td,ed->te', normed, weight, preferred_element_type=jnp.float32)]
    ppermute x22 -> x0, starting transfers between devices: 133 us -> none  [from_behind(): lax.ppermute(value, axis, [(source, source + steps) for source in range(f...]
    pallas_call x0 -> x1, Pallas kernels: none -> 111 us  [pipeline(): pl.pallas_call(pipeline_kernel, name='pipeline', out_shape=jax.ShapeDtype...]
    dynamic_update_slice x24 -> x0, local copies, waits for them, and re-layouts: 86.5 us -> none  [the longest x12 43.6 us: block_layer(): key_rows = lax.dynamic_update_slice_in_dim(key_cache, key_new, offset, 0)]
    all_gather x2 -> x1, waiting for transfers between devices: 182 us -> 106 us  [local(): weights = lax.all_gather(shard, 'dp', axis=1, tiled=True)]
    reduce_scatter x1, waiting for transfers between devices: 305 us -> 239 us  [local(): lax.psum_scatter(grad.astype(jnp.float32), 'dp', scatter_dimension=0, til...]
    add x22 -> x0, other arithmetic: 55.6 us -> none  [backward_step(): return (d_inputs, key_grad + d_keys, value_grad + d_values, extra)]
  transfers between devices with their start and end apart: 25 -> 2, of which waited for: 25 -> 2; matrix products, arithmetic and copies ran while one was open for 2% -> 0% of each run, Pallas kernels for 0% -> 0%
where the time goes in v1:
time: 480 us; the launch traced here: 476 us
  waiting for transfers between devices  345 us (72%)
  Pallas kernels  111 us (23%)
  between operations  13.4 us (3%)
  other arithmetic  4.81 us (1%)
    reduce_scatter x1, waiting for transfers between devices, local(): lax.psum_scatter(grad.astype(jnp.float32), 'dp', scatter_dimension=0, til...  239 us
    pallas_call x1, Pallas kernels, pipeline(): pl.pallas_call(pipeline_kernel, name='pipeline', out_shape=jax.ShapeDtype...  111 us
    all_gather x1, waiting for transfers between devices, local(): weights = lax.all_gather(shard, 'dp', axis=1, tiled=True)  106 us
  transfers between devices with their start and end apart: 2, of which 2 were waited for; matrix products, arithmetic and copies ran while one was open for 0% of the time, Pallas kernels for 0%

profile of v1, /device:TPU:1, one launch (start us, length us, event | category | flops | bytes accessed | tf_op | source)
XLA Modules:
  0.0 476.2 jit_solution(8547505550914146758)
XLA Ops:
  6.5 0.0 all-gather.2.cloned.1.call-start
  6.5 1.6 pad_maximum_fusion
  8.1 0.0 all-gather.2.cloned.1.call-update
  8.1 0.0 reduce-scatter.2.cloned.1.call-start
  8.2 0.9 fusion.1.bias_ref
  9.0 106.2 %all-gather.2.cloned.1.call-done.w_ref = bf16[4,1024,1024]{2,1,0:T(8,128)(2,1)} async-done(((bf16[4,16,1024]{2,1,0:T(8,128)(2,1)}), bf16[4,1024,1024]{2,1,0:T(8,128)(2,1)}) %all-gather.2.cloned.1.call-update) | async-done | bytes 8388624 | tf_op jit(solution)/shard_map/all_gather | solution.py:180
  115.3 0.0 copy-start
  115.3 1.0 copy-done
  116.3 0.0 copy-start.1
  116.3 1.0 copy-done.1
  117.3 110.9 %pipeline.1 = bf16[1024,1024]{1,0:T(8,128)(2,1)S(1)} custom-call(bf16[192,1024]{1,0:T(8,128)(2,1)S(1)} %bitcast.5, bf16[192,1024]{1,0:T(8,128)(2,1)S(1)} %bitcast.6, f32[192,192]{1,0:T(8,128)S(1)} %fusion.1.bias_ref, bf16[4,1024,1024]{2,1,0:T(8,128)(2,1)} %all-gather.2.cloned.1.call-done.w_ref), custom_call_target="tpu_custom_call" | custom-call | tf_op jit(solution)/shard_map/pipeline/pallas_call | solution.py:157
  228.1 2.4 convert_element_type.3
  230.5 0.0 reduce-scatter.2.cloned.1.call-update
  230.6 238.8 %reduce-scatter.2.cloned.1.call-done = f32[16,1024]{1,0:T(8,128)} async-done(((f32[1024,1024]{1,0:T(8,128)}), f32[16,1024]{1,0:T(8,128)}) %reduce-scatter.2.cloned.1.call-update) | async-done | bytes 65552 | tf_op jit(solution)/shard_map/reduce_scatter | solution.py:189
Async XLA Ops:
  6.5 108.7 %all-gather.2.cloned.1.call-start = ((), (), s32[]{:S(2)}) async-start(), calls=%async_computation.1 | async-start | bytes 8519680 | tf_op jit(solution)/shard_map/all_gather | solution.py:180
  8.1 461.2 %reduce-scatter.2.cloned.1.call-start = ((), (), s32[]{:S(2)}) async-start(), calls=%async_computation.2 | async-start | bytes 4259840 | tf_op jit(solution)/shard_map/reduce_scatter | solution.py:189
  115.3 1.0 copy-start
  116.3 1.0 copy-start.1
Sparse Core Ops, SparseCore 0:
  10.4 104.7 all-gather.1
  230.7 238.6 reduce-scatter.1

commit v2 on v1

--- a/solution.py
+++ b/solution.py
@@ -13,6 +13,7 @@
 PAIR = 2 * HEAD_DIM
 NC = 2
 SECTIONS = 8
+RING = 8
 epsilon = 1e-05
 masked_score = -1e30
 
@@ -30,8 +31,69 @@
     return jnp.concatenate([jnp.where(low, block, zero), jnp.where(low, zero, block)], axis=0)
 
 
+def gather_copy(w_ref, sends, recvs, phase, j, way, step):
+    d = lax.axis_index("dp")
+    y, z = d // RING, lax.rem(d, RING)
+    along_z = (j < 2) == (phase == 0)
+    me = z if along_z else y
+    block = lax.rem(me - way * (step - 1) + RING, RING)
+    other = lax.rem(me + way + RING, RING)
+    other = y * RING + other if along_z else other * RING + z
+    if phase == 0:
+        ref = w_ref.at[j, y, block] if along_z else w_ref.at[j, block, z]
+    else:
+        ref = w_ref.at[j, :, block] if along_z else w_ref.at[j, block]
+    bit = (1 - way) // 2
+    return pltpu.make_async_remote_copy(
+        src_ref=ref, dst_ref=ref, send_sem=sends.at[phase, j, bit, step - 1],
+        recv_sem=recvs.at[phase, j, bit, step - 1], device_id={"dp": other}, device_id_type=MESH,
+    )
+
+
+def gather_steps(j, way):
+    return RING // 2 if (way == 1) == (j % 2 == 0) else RING // 2 - 1
+
+
+STREAMS = [(j, way) for j in range(4) for way in (1, -1)]
+
+
+def gather(w_ref, sends, recvs):
+    for phase in range(2):
+        for j, way in STREAMS:
+            gather_copy(w_ref, sends, recvs, phase, j, way, 1).start()
+        for step in range(1, RING // 2 + 1):
+            for j, way in STREAMS:
+                if step <= gather_steps(j, way):
+                    gather_copy(w_ref, sends, recvs, phase, j, way, step).wait_recv()
+                if step < gather_steps(j, way):
+                    gather_copy(w_ref, sends, recvs, phase, j, way, step + 1).start()
+
+
+def gather_end(w_ref, sends, recvs):
+    for phase in range(2):
+        for j, way in STREAMS:
+            for step in range(1, gather_steps(j, way) + 1):
+                gather_copy(w_ref, sends, recvs, phase, j, way, step).wait_send()
+
+
+ORDER = (4, 3, 5, 2, 6, 1, 7)
+
+
+def scatter_copy(src, dst, send, recv, along_z, k):
+    d = lax.axis_index("dp")
+    y, z = d // RING, lax.rem(d, RING)
+    place = lax.rem((z if along_z else y) + k, RING)
+    other = y * RING + place if along_z else place * RING + z
+    return pltpu.make_async_remote_copy(
+        src_ref=src(place), dst_ref=dst.at[k - 1], send_sem=send.at[k - 1], recv_sem=recv.at[k - 1],
+        device_id={"dp": other}, device_id_type=MESH,
+    )
+
+
 def pipeline_kernel(
-    x_ref, cot_ref, bias_ref, w_ref, dw_ref,
+    x_ref, cot_ref, bias_ref, attn_ref, out_ref, o_ref,
+    w_ref, dw, landa, landb, parta, partb, enda, endb,
+    gsend, grecv, rsend, rrecv,
     hid, outb, gin, gout, qb, kb, vb, mixb, pb, dmb, dqb, dkb, dvb,
     fsend, frecv, bsend, brecv,
 ):
@@ -40,10 +102,20 @@
     rows_c = length // NC
     barrier = pltpu.get_barrier_semaphore()
 
+    d = lax.axis_index("dp")
+    y, z = d // RING, lax.rem(d, RING)
     for step in (1, SECTIONS - 1):
         other = lax.rem(s + step, SECTIONS)
         pl.semaphore_signal(barrier, inc=1, device_id={"section": other}, device_id_type=MESH)
-    pl.semaphore_wait(barrier, 2)
+    for step in range(1, RING):
+        for other in (lax.rem(y + step, RING) * RING + z, y * RING + lax.rem(z + step, RING)):
+            pl.semaphore_signal(barrier, inc=1, device_id={"dp": other}, device_id_type=MESH)
+    for j in range(3):
+        w_ref[j, y, z] = attn_ref[j]
+    w_ref[3, y, z] = out_ref[...]
+    pl.semaphore_wait(barrier, 2 + 2 * (RING - 1))
+    gather(w_ref, gsend, grecv)
+    weight = lambda j: w_ref[j].reshape(width, width)
 
     def forward_copy(c):
         rows = pl.ds(c * rows_c, rows_c)
@@ -82,7 +154,7 @@
         r = lax.rsqrt(jnp.mean(h * h, axis=-1, keepdims=True) + epsilon)
         normed = (h * r).astype(jnp.bfloat16)
         for j, buf in ((0, qb), (1, kb), (2, vb)):
-            buf[lo:hi] = dot(normed, w_ref[j], NT).astype(jnp.bfloat16)
+            buf[lo:hi] = dot(normed, weight(j), NT).astype(jnp.bfloat16)
         bias = bias_ref[lo:hi, :hi]
         bias2 = jnp.concatenate([bias, bias], axis=0)
         for p in range(PAIRS):
@@ -98,7 +170,7 @@
 
         @pl.when(s < SECTIONS - 1)
         def _():
-            added = hid[lo:hi].astype(jnp.float32) + dot(mixb[lo:hi], w_ref[3], NT)
+            added = hid[lo:hi].astype(jnp.float32) + dot(mixb[lo:hi], weight(3), NT)
             outb[lo:hi] = added.astype(jnp.bfloat16)
             forward_copy(c).start()
 
@@ -112,7 +184,7 @@
         @pl.when(s > 0)
         def _():
             g = gin[lo:hi]
-            dmb[...] = dot(g, w_ref[3], NN).astype(jnp.bfloat16)
+            dmb[...] = dot(g, weight(3), NN).astype(jnp.bfloat16)
             for p in range(PAIRS):
                 cols = slice(p * PAIR, (p + 1) * PAIR)
                 d01 = halves(dmb[:, cols], low)
@@ -126,9 +198,9 @@
                 dqb[:, cols] = jnp.where(low, dq01[:rows_c], dq01[rows_c:]).astype(jnp.bfloat16)
                 dkb[:hi, cols] += dot(ds, q01, TN)
                 dvb[:hi, cols] += dot(weights, d01, TN)
-            dn = dot(dqb[...], w_ref[0], NN)
-            dn += dot(dkb[lo:hi].astype(jnp.bfloat16), w_ref[1], NN)
-            dn += dot(dvb[lo:hi].astype(jnp.bfloat16), w_ref[2], NN)
+            dn = dot(dqb[...], weight(0), NN)
+            dn += dot(dkb[lo:hi].astype(jnp.bfloat16), weight(1), NN)
+            dn += dot(dvb[lo:hi].astype(jnp.bfloat16), weight(2), NN)
             h = hid[lo:hi].astype(jnp.float32)
             r = lax.rsqrt(jnp.mean(h * h, axis=-1, keepdims=True) + epsilon)
             along = jnp.mean(dn * h, axis=-1, keepdims=True)
@@ -136,10 +208,50 @@
             gout[lo:hi] = (g.astype(jnp.float32) + dh).astype(jnp.bfloat16)
             backward_copy(c).start()
 
-    step = 256
-    for j in range(0, width, step):
-        dw_ref[j : j + step] = dot(gin[:, j : j + step], mixb[...], TN).astype(jnp.bfloat16)
-
+    half = width // 2
+
+    def grad_block(place):
+        cols = pl.ds(pl.multiple_of(place * (width // RING), width // RING), width // RING)
+        block = dot(gin[:, cols], mixb[...], TN).astype(jnp.bfloat16)
+        dw[pl.ds(place, 1)] = block.reshape(1, RING, width // RING // RING, width)
+
+    first = {
+        False: functools.partial(scatter_copy, lambda p: dw.at[p, :, :, :half], landa, rsend.at[0], rrecv.at[0], False),
+        True: functools.partial(scatter_copy, lambda p: dw.at[:, p, :, half:], landb, rsend.at[1], rrecv.at[1], True),
+    }
+    second = {
+        True: functools.partial(scatter_copy, lambda p: parta.at[p], enda, rsend.at[2], rrecv.at[2], True),
+        False: functools.partial(scatter_copy, lambda p: partb.at[p], endb, rsend.at[3], rrecv.at[3], False),
+    }
+    for k in ORDER:
+        grad_block(lax.rem(y + k, RING))
+        first[False](k).start()
+    grad_block(y)
+    for k in ORDER:
+        first[True](k).start()
+
+    for along_z, own, land, part in ((False, dw[y, :, :, :half], landa, parta), (True, dw[:, z, :, half:], landb, partb)):
+        total = own.astype(jnp.float32)
+        for k in ORDER:
+            first[along_z](k).wait_recv()
+            total += land[k - 1].astype(jnp.float32)
+        part[...] = total.astype(jnp.bfloat16)
+        for k in ORDER:
+            second[not along_z](k).start()
+    for along_z, part, mine, land, cols in (
+        (True, parta, z, enda, slice(0, half)), (False, partb, y, endb, slice(half, width))
+    ):
+        total = part[mine].astype(jnp.float32)
+        for k in ORDER:
+            second[along_z](k).wait_recv()
+            total += land[k - 1].astype(jnp.float32)
+        o_ref[:, cols] = total
+
+    for k in ORDER:
+        for along_z in (False, True):
+            first[along_z](k).wait_send()
+            second[along_z](k).wait_send()
+    gather_end(w_ref, gsend, grecv)
     for c in range(NC):
         @pl.when(s < SECTIONS - 1)
         def _():
@@ -150,17 +262,29 @@
             backward_copy(c).wait_send()
 
 
-def pipeline(context, cot, bias, weights):
+def pipeline(context, cot, bias, attn, out):
     length, width = context.shape
     rows_c = length // NC
+    own = out.shape[0]
     full = pltpu.VMEM((length, width), jnp.bfloat16)
+    landing = pltpu.VMEM((RING - 1, RING, own, width // 2), jnp.bfloat16)
+    part = pltpu.VMEM((RING, own, width // 2), jnp.bfloat16)
+    end = pltpu.VMEM((RING - 1, own, width // 2), jnp.bfloat16)
     return pl.pallas_call(
         pipeline_kernel,
         name="pipeline",
-        out_shape=jax.ShapeDtypeStruct((width, width), jnp.bfloat16),
-        in_specs=[pl.BlockSpec(memory_space=pltpu.VMEM)] * 4,
+        out_shape=jax.ShapeDtypeStruct((own, width), jnp.float32),
+        in_specs=[pl.BlockSpec(memory_space=pltpu.VMEM)] * 5,
         out_specs=pl.BlockSpec(memory_space=pltpu.VMEM),
-        scratch_shapes=[full] * 8 + [
+        scratch_shapes=[
+            pltpu.VMEM((4, RING, RING, own, width), jnp.bfloat16),
+            pltpu.VMEM((RING, RING, own, width), jnp.bfloat16),
+            landing, landing, part, part, end, end,
+            pltpu.SemaphoreType.DMA((2, 4, 2, RING // 2)),
+            pltpu.SemaphoreType.DMA((2, 4, 2, RING // 2)),
+            pltpu.SemaphoreType.DMA((4, RING - 1)),
+            pltpu.SemaphoreType.DMA((4, RING - 1)),
+        ] + [full] * 8 + [
             pltpu.VMEM((NC, PAIRS, 2 * rows_c, length), jnp.bfloat16),
             pltpu.VMEM((rows_c, width), jnp.bfloat16),
             pltpu.VMEM((rows_c, width), jnp.bfloat16),
@@ -170,14 +294,11 @@
         compiler_params=pltpu.CompilerParams(
             collective_id=1, has_side_effects=True, vmem_limit_bytes=48 << 20
         ),
-    )(context, cot, bias, weights)
+    )(context, cot, bias, attn, out)
 
 
 def local(hidden_in, cotangent, segments, attn_weights, out_weight):
-    width = out_weight.shape[-1]
     section_index = lax.axis_index("section")
-    shard = jnp.concatenate([attn_weights[0], out_weight], axis=0)
-    weights = lax.all_gather(shard, "dp", axis=1, tiled=True)
     context = hidden_in[0]
     length = context.shape[0]
     positions = jnp.arange(length, dtype=jnp.int32)
@@ -185,9 +306,7 @@
     same_segment = segments[0][:, None] == segments[0][None, :]
     allowed = causal & (same_segment | (section_index % 2 == 1))
     bias = jnp.where(allowed, 0.0, masked_score).astype(jnp.float32)
-    grad = pipeline(context, cotangent[0], bias, weights)
-    result = lax.psum_scatter(grad.astype(jnp.float32), "dp", scatter_dimension=0, tiled=True)
-    return result[None]
+    return pipeline(context, cotangent[0], bias, attn_weights[0], out_weight[0])[None]
 
 
 def solution(mesh):

time: 480 us -> 214 us (0.45)
  waiting for transfers between devices: 345 us -> 0 us
  Pallas kernels: 111 us -> 209 us
  between operations: 13.4 us -> 0.02 us
    reduce_scatter x1 -> x0, waiting for transfers between devices: 239 us -> none  [local(): lax.psum_scatter(grad.astype(jnp.float32), 'dp', scatter_dimension=0, til...]
    all_gather x1 -> x0, waiting for transfers between devices: 106 us -> none  [local(): weights = lax.all_gather(shard, 'dp', axis=1, tiled=True)]
    pallas_call x1, Pallas kernels: 111 us -> 209 us  [pipeline(): pl.pallas_call(pipeline_kernel, name='pipeline', out_shape=jax.ShapeDtype...]
  transfers between devices with their start and end apart: 2 -> 0, of which waited for: 2 -> 0; matrix products, arithmetic and copies ran while one was open for 0% -> 0% of each run, Pallas kernels for 0% -> 0%
where the time goes in v2:
time: 214 us; the launch traced here: 213 us
  Pallas kernels  209 us (98%)
  local copies, waits for them, and re-layouts  4.09 us (2%)
    pallas_call x1, Pallas kernels, pipeline(): pl.pallas_call(pipeline_kernel, name='pipeline', out_shape=jax.ShapeDtype...  209 us

profile of v2, /device:TPU:1, one launch (start us, length us, event | category | flops | bytes accessed | tf_op | source)
XLA Modules:
  0.0 213.3 jit_solution(14159759675939800053)
XLA Ops:
  0.0 0.0 copy-start.4
  0.0 0.7 copy-done.4
  0.7 0.0 copy-start.2
  0.7 0.0 copy-start.3
  0.7 0.1 fusion.1.bias_ref
  0.8 0.8 copy-done.2
  1.6 0.0 copy-done.3
  1.6 0.0 copy-start
  1.6 1.0 copy-done
  2.6 0.0 copy-start.1
  2.6 1.0 copy-done.1
  3.6 209.1 %pipeline.1 = f32[16,1024]{1,0:T(8,128)S(1)} custom-call(bf16[192,1024]{1,0:T(8,128)(2,1)S(1)} %bitcast.6, bf16[192,1024]{1,0:T(8,128)(2,1)S(1)} %bitcast.7, f32[192,192]{1,0:T(8,128)S(1)} %fusion.1.bias_ref, bf16[3,16,1024]{2,1,0:T(8,128)(2,1)S(1)} %bitcast.9, bf16[16,1024]{1,0:T(8,128)(2,1)S(1)} %bitcast.10), custom_call_target="tpu_custom_call" | custom-call | tf_op jit(solution)/shard_map/pipeline/pallas_call | solution.py:273
  212.7 0.6 copy.7
Async XLA Ops:
  0.0 0.7 copy-start.4
  0.7 0.9 copy-start.2
  0.7 0.9 copy-start.3
  1.6 1.0 copy-start
  2.6 1.0 copy-start.1

commit v3 on v1

v3 whole, which is shorter than its diff:
```python
import functools
import jax
import jax.numpy as jnp
from jax import lax
from jax.experimental import pallas as pl
from jax.experimental.pallas import tpu as pltpu
from jax.sharding import PartitionSpec as P

MESH = pl.DeviceIdType.MESH
HEADS = 16
HEAD_DIM = 64
PAIRS = HEADS // 2
PAIR = 2 * HEAD_DIM
NC = 2
SECTIONS = 8
RING = 8
epsilon = 1e-05
masked_score = -1e30

NT = (((1,), (1,)), ((), ()))
NN = (((1,), (0,)), ((), ()))
TN = (((0,), (0,)), ((), ()))


def dot(a, b, dims):
    return lax.dot_general(a, b, dims, preferred_element_type=jnp.float32)


def halves(block, low):
    zero = jnp.zeros_like(block)
    return jnp.concatenate([jnp.where(low, block, zero), jnp.where(low, zero, block)], axis=0)


def first_steps(kind, way):
    return RING // 2 if (way == 1) == (kind == 0) else RING // 2 - 1


def second_steps(a, way):
    return RING // 2 if (way == 1) == (a % 2 == 0) else RING // 2 - 1


def place():
    d = lax.axis_index("dp")
    return d // RING, lax.rem(d, RING)


def around(me, step):
    return lax.rem(me + step + 2 * RING, RING)


def block_copy(w_ref, kind, y, z, other, send, recv):
    ref = w_ref.at[2 * kind : 2 * kind + 2, y, z]
    return pltpu.make_async_remote_copy(
        src_ref=ref, dst_ref=ref, send_sem=send, recv_sem=recv, device_id={"dp": other}, device_id_type=MESH
    )


def first_copy(w_ref, sends, recvs, kind, way, step):
    y, z = place()
    sems = sends.at[kind, (1 - way) // 2, step - 1], recvs.at[kind, (1 - way) // 2, step - 1]
    if kind == 0:
        return block_copy(w_ref, kind, y, around(z, -way * (step - 1)), y * RING + around(z, way), *sems)
    return block_copy(w_ref, kind, around(y, -way * (step - 1)), z, around(y, way) * RING + z, *sems)


def second_copy(w_ref, sends, recvs, kind, a, way, step):
    y, z = place()
    sems = sends.at[kind, a + 4, (1 - way) // 2, step - 1], recvs.at[kind, a + 4, (1 - way) // 2, step - 1]
    if kind == 0:
        return block_copy(
            w_ref, kind, around(y, -way * (step - 1)), around(z, a), around(y, way) * RING + z, *sems
        )
    return block_copy(w_ref, kind, around(y, a), around(z, -way * (step - 1)), y * RING + around(z, way), *sems)


def offsets(kind):
    return [0, -1, 1, -2, 2, -3, 3, 4 if kind == 1 else -4]


WAYS = (1, -1)


def gather(w_ref, send1, recv1, send2, recv2, beside):
    first = functools.partial(first_copy, w_ref, send1, recv1)
    second = functools.partial(second_copy, w_ref, send2, recv2)
    for kind in range(2):
        for way in WAYS:
            first(kind, way, 1).start()
    for kind in range(2):
        for way in WAYS:
            second(kind, 0, way, 1).start()
    for wave in range(1, RING + 1):
        for kind in range(2):
            for way in WAYS:
                if wave <= first_steps(kind, way):
                    first(kind, way, wave).wait_recv()
                    if wave < first_steps(kind, way):
                        first(kind, way, wave + 1).start()
                    for onward in WAYS:
                        second(kind, -way * wave, onward, 1).start()
        for a_index in range(RING):
            for kind in range(2):
                a = offsets(kind)[a_index]
                step = wave - abs(a)
                for way in WAYS:
                    if 1 <= step <= second_steps(a, way):
                        second(kind, a, way, step).wait_recv()
                        if step < second_steps(a, way):
                            second(kind, a, way, step + 1).start()
        beside(wave)


def gather_end(w_ref, send1, recv1, send2, recv2):
    for kind in range(2):
        for way in WAYS:
            for step in range(1, first_steps(kind, way) + 1):
                first_copy(w_ref, send1, recv1, kind, way, step).wait_send()
            for a in offsets(kind):
                for step in range(1, second_steps(a, way) + 1):
                    second_copy(w_ref, send2, recv2, kind, a, way, step).wait_send()


ORDER = (4, 3, 5, 2, 6, 1, 7)


def spread_copy(src, dst, send, recv, along_z, k):
    y, z = place()
    there = around(z if along_z else y, k)
    other = y * RING + there if along_z else there * RING + z
    return pltpu.make_async_remote_copy(
        src_ref=src(there), dst_ref=dst, send_sem=send.at[k - 1], recv_sem=recv.at[k - 1],
        device_id={"dp": other}, device_id_type=MESH,
    )


def pipeline_kernel(
    x_ref, cot_ref, seg_ref, attn_ref, out_ref, o_ref,
    w_ref, bias_ref, swap, gswap, mixes, gs, parts, ends,
    gsend1, grecv1, gsend2, grecv2, msend, mrecv, csend, crecv, esend, erecv, lsem,
    hid, outb, gin, gout, qb, kb, vb, mixb, pb, dmb, dqb, dkb, dvb,
    fsend, frecv, bsend, brecv,
):
    s = lax.axis_index("section")
    y, z = place()
    length, width = x_ref.shape
    rows_c = length // NC
    half = width // 2
    slice_cols = width // RING
    barrier = pltpu.get_barrier_semaphore()
    for step in (1, SECTIONS - 1):
        other = lax.rem(s + step, SECTIONS)
        pl.semaphore_signal(barrier, inc=1, device_id={"section": other}, device_id_type=MESH)
    for step in range(1, RING):
        for other in (around(y, step) * RING + z, y * RING + around(z, step)):
            pl.semaphore_signal(barrier, inc=1, device_id={"dp": other}, device_id_type=MESH)
    shard = [pltpu.make_async_copy(attn_ref.at[j], w_ref.at[j, y, z], lsem.at[j]) for j in range(3)]
    shard.append(pltpu.make_async_copy(out_ref, w_ref.at[3, y, z], lsem.at[3]))
    for copy in shard:
        copy.start()
    in_copy = pltpu.make_async_copy(x_ref, hid, lsem.at[4])
    cot_copy = pltpu.make_async_copy(cot_ref, gin, lsem.at[4])

    @pl.when(s == 0)
    def _():
        in_copy.start()

    @pl.when(s == SECTIONS - 1)
    def _():
        cot_copy.start()

    for copy in shard:
        copy.wait()
    pl.semaphore_wait(barrier, 2 + 2 * (RING - 1))
    own = slice_cols // RING

    def mask():
        ids = lax.broadcasted_iota(jnp.int32, (32, length), 0)
        one_hot = jnp.where(ids == seg_ref[...], 1.0, 0.0).astype(jnp.bfloat16)
        same = dot(one_hot, one_hot, TN) > 0.5
        query = lax.broadcasted_iota(jnp.int32, (length, length), 0)
        key = lax.broadcasted_iota(jnp.int32, (length, length), 1)
        any_segment = lax.broadcast(lax.rem(s, 2), (length, length)) == 1
        allowed = (key <= query) & (same | any_segment)
        bias_ref[...] = jnp.where(allowed, 0.0, masked_score)
        dkb[...] = jnp.zeros_like(dkb)
        dvb[...] = jnp.zeros_like(dvb)

    def swap_rows(j):
        row = lax.broadcasted_iota(jnp.int32, (slice_cols, width), 0) + j * slice_cols
        col = lax.broadcasted_iota(jnp.int32, (slice_cols, width), 1)
        source = lax.rem(col, slice_cols) // own * slice_cols + col // slice_cols * own + lax.rem(col, own)
        swap[j * slice_cols : (j + 1) * slice_cols] = jnp.where(row == source, 1.0, 0.0).astype(jnp.bfloat16)

    def beside(wave):
        swap_rows(wave - 1)
        if wave == 4:
            mask()

    gather(w_ref, gsend1, grecv1, gsend2, grecv2, beside)

    @pl.when(s == 0)
    def _():
        in_copy.wait()

    @pl.when(s == SECTIONS - 1)
    def _():
        cot_copy.wait()

    weight = lambda j: w_ref[j].reshape(width, width)

    def forward_copy(c):
        rows = pl.ds(c * rows_c, rows_c)
        return pltpu.make_async_remote_copy(
            src_ref=outb.at[rows], dst_ref=hid.at[rows], send_sem=fsend.at[c], recv_sem=frecv.at[c],
            device_id={"section": jnp.minimum(s + 1, SECTIONS - 1)}, device_id_type=MESH,
        )

    def backward_copy(c):
        rows = pl.ds(c * rows_c, rows_c)
        return pltpu.make_async_remote_copy(
            src_ref=gout.at[rows], dst_ref=gin.at[rows], send_sem=bsend.at[c], recv_sem=brecv.at[c],
            device_id={"section": jnp.maximum(s - 1, 0)}, device_id_type=MESH,
        )

    low = lax.broadcasted_iota(jnp.int32, (rows_c, PAIR), 1) < HEAD_DIM

    for c in range(NC):
        lo, hi = c * rows_c, (c + 1) * rows_c

        @pl.when(s > 0)
        def _():
            forward_copy(c).wait_recv()

        h = hid[lo:hi].astype(jnp.float32)
        r = lax.rsqrt(jnp.mean(h * h, axis=-1, keepdims=True) + epsilon)
        normed = (h * r).astype(jnp.bfloat16)
        for j, buf in ((0, qb), (1, kb), (2, vb)):
            buf[lo:hi] = dot(normed, weight(j), NT).astype(jnp.bfloat16)
        bias = bias_ref[lo:hi, :hi]
        bias2 = jnp.concatenate([bias, bias], axis=0)
        for p in range(PAIRS):
            cols = slice(p * PAIR, (p + 1) * PAIR)
            q01 = halves(qb[lo:hi, cols], low)
            scores = dot(q01, kb[:hi, cols], NT) * HEAD_DIM ** (-0.5) + bias2
            top = jnp.max(scores, axis=-1, keepdims=True)
            e = jnp.exp(scores - top)
            weights = (e / jnp.sum(e, axis=-1, keepdims=True)).astype(jnp.bfloat16)
            pb[c, p, :, :hi] = weights
            o = dot(weights, vb[:hi, cols], NN)
            mixb[lo:hi, cols] = jnp.where(low, o[:rows_c], o[rows_c:]).astype(jnp.bfloat16)

        @pl.when(s < SECTIONS - 1)
        def _():
            added = hid[lo:hi].astype(jnp.float32) + dot(mixb[lo:hi], weight(3), NT)
            outb[lo:hi] = added.astype(jnp.bfloat16)
            forward_copy(c).start()

    def mix_copy(along_z, k):
        cols = pl.ds(half if along_z else 0, half)
        return spread_copy(
            lambda there: mixb.at[:, cols], mixes.at[int(along_z), k], msend.at[int(along_z)],
            mrecv.at[int(along_z)], along_z, k,
        )

    def grad_copy(c, along_z, k):
        rows = pl.ds(c * rows_c, rows_c)
        source = gswap if along_z else gin
        return spread_copy(
            lambda there: source.at[rows, pl.ds(pl.multiple_of(there * slice_cols, slice_cols), slice_cols)],
            gs.at[int(along_z), k, rows], csend.at[int(along_z), c], crecv.at[int(along_z), c], along_z, k,
        )

    def end_copy(along_z, k):
        return spread_copy(
            lambda there: parts.at[int(not along_z), there], ends.at[int(not along_z), k - 1],
            esend.at[int(not along_z)], erecv.at[int(not along_z)], along_z, k,
        )

    for k in ORDER:
        for along_z in (False, True):
            mix_copy(along_z, k).start()

    for c in reversed(range(NC)):
        lo, hi = c * rows_c, (c + 1) * rows_c

        @pl.when(s < SECTIONS - 1)
        def _():
            backward_copy(c).wait_recv()

        @pl.when(s > 0)
        def _():
            g = gin[lo:hi]
            dmb[...] = dot(g, weight(3), NN).astype(jnp.bfloat16)
            for p in range(PAIRS):
                cols = slice(p * PAIR, (p + 1) * PAIR)
                d01 = halves(dmb[:, cols], low)
                q01 = halves(qb[lo:hi, cols], low)
                weights = pb[c, p, :, :hi]
                wide = weights.astype(jnp.float32)
                dweights = dot(d01, vb[:hi, cols], NT)
                delta = jnp.sum(wide * dweights, axis=-1, keepdims=True)
                ds = (wide * (dweights - delta) * HEAD_DIM ** (-0.5)).astype(jnp.bfloat16)
                dq01 = dot(ds, kb[:hi, cols], NN)
                dqb[:, cols] = jnp.where(low, dq01[:rows_c], dq01[rows_c:]).astype(jnp.bfloat16)
                dkb[:hi, cols] += dot(ds, q01, TN)
                dvb[:hi, cols] += dot(weights, d01, TN)
            dn = dot(dqb[...], weight(0), NN)
            dn += dot(dkb[lo:hi].astype(jnp.bfloat16), weight(1), NN)
            dn += dot(dvb[lo:hi].astype(jnp.bfloat16), weight(2), NN)
            h = hid[lo:hi].astype(jnp.float32)
            r = lax.rsqrt(jnp.mean(h * h, axis=-1, keepdims=True) + epsilon)
            along = jnp.mean(dn * h, axis=-1, keepdims=True)
            dh = dn * r - h * (r * r * r * along)
            gout[lo:hi] = (g.astype(jnp.float32) + dh).astype(jnp.bfloat16)
            backward_copy(c).start()

        for k in ORDER:
            grad_copy(c, False, k).start()
        gswap[lo:hi] = dot(gin[lo:hi], swap[...], NN).astype(jnp.bfloat16)
        for k in ORDER:
            grad_copy(c, True, k).start()

    for along_z in (False, True):
        i, me, source = int(along_z), (z if along_z else y), (gswap if along_z else gin)
        mixes[i, 0] = mixb[:, i * half : (i + 1) * half]
        gs[i, 0] = source[:, pl.ds(pl.multiple_of(me * slice_cols, slice_cols), slice_cols)]
        for k in ORDER:
            mix_copy(along_z, k).wait_recv()
            for c in range(NC):
                grad_copy(c, along_z, k).wait_recv()
        total = dot(
            gs[i].reshape(RING * length, slice_cols), mixes[i].reshape(RING * length, half), TN
        )
        parts[i] = total.astype(jnp.bfloat16).reshape(RING, own, half)
        for k in ORDER:
            end_copy(not along_z, k).start()
    for along_z in (False, True):
        i, me = int(along_z), (y if along_z else z)
        total = parts[i, me].astype(jnp.float32)
        for k in ORDER:
            end_copy(not along_z, k).wait_recv()
            total += ends[i, k - 1].astype(jnp.float32)
        o_ref[:, i * half : (i + 1) * half] = total

    for along_z in (False, True):
        for k in ORDER:
            mix_copy(along_z, k).wait_send()
            end_copy(along_z, k).wait_send()
            for c in range(NC):
                grad_copy(c, along_z, k).wait_send()
    gather_end(w_ref, gsend1, grecv1, gsend2, grecv2)
    for c in range(NC):
        @pl.when(s < SECTIONS - 1)
        def _():
            forward_copy(c).wait_send()

        @pl.when(s > 0)
        def _():
            backward_copy(c).wait_send()


def local(hidden_in, cotangent, segments, attn_weights, out_weight):
    length, width = hidden_in.shape[1:]
    own = out_weight.shape[1]
    rows_c = length // NC
    half = width // 2
    full = pltpu.VMEM((length, width), jnp.bfloat16)
    dma = lambda *shape: pltpu.SemaphoreType.DMA(shape)
    anywhere = pl.BlockSpec(memory_space=pl.ANY)
    result = pl.pallas_call(
        pipeline_kernel,
        name="pipeline",
        out_shape=jax.ShapeDtypeStruct((own, width), jnp.float32),
        in_specs=[anywhere, anywhere, pl.BlockSpec(memory_space=pltpu.VMEM), anywhere, anywhere],
        out_specs=pl.BlockSpec(memory_space=pltpu.VMEM),
        scratch_shapes=[
            pltpu.VMEM((4, RING, RING, own, width), jnp.bfloat16),
            pltpu.VMEM((length, length), jnp.float32),
            pltpu.VMEM((width, width), jnp.bfloat16),
            full,
            pltpu.VMEM((2, RING, length, half), jnp.bfloat16),
            pltpu.VMEM((2, RING, length, width // RING), jnp.bfloat16),
            pltpu.VMEM((2, RING, own, half), jnp.bfloat16),
            pltpu.VMEM((2, RING - 1, own, half), jnp.bfloat16),
            dma(2, 2, 4), dma(2, 2, 4), dma(2, 9, 2, 4), dma(2, 9, 2, 4),
            dma(2, RING - 1), dma(2, RING - 1), dma(2, NC, RING - 1), dma(2, NC, RING - 1),
            dma(2, RING - 1), dma(2, RING - 1), dma(5),
        ] + [full] * 8 + [
            pltpu.VMEM((NC, PAIRS, 2 * rows_c, length), jnp.bfloat16),
            pltpu.VMEM((rows_c, width), jnp.bfloat16),
            pltpu.VMEM((rows_c, width), jnp.bfloat16),
            pltpu.VMEM((length, width), jnp.float32),
            pltpu.VMEM((length, width), jnp.float32),
        ] + [dma(NC)] * 4,
        compiler_params=pltpu.CompilerParams(
            collective_id=1, has_side_effects=True, vmem_limit_bytes=56 << 20
        ),
    )(hidden_in[0], cotangent[0], segments, attn_weights[0], out_weight[0])
    return result[None]


def solution(mesh):
    in_specs = (
        P("dp", None, None),
        P("dp", None, None),
        P("dp", None),
        P("section", None, "dp", None),
        P("section", "dp", None),
    )
    return jax.shard_map(
        local, mesh=mesh, in_specs=in_specs, out_specs=P("section", "dp", None), check_vma=False
    )
```

time: 480 us -> 190 us (0.40)
  waiting for transfers between devices: 345 us -> 0 us
  Pallas kernels: 111 us -> 188 us
  between operations: 13.4 us -> 0.01 us
  other arithmetic: 4.81 us -> 0 us
    reduce_scatter x1 -> x0, waiting for transfers between devices: 239 us -> none  [local(): lax.psum_scatter(grad.astype(jnp.float32), 'dp', scatter_dimension=0, til...]
    all_gather x1 -> x0, waiting for transfers between devices: 106 us -> none  [local(): weights = lax.all_gather(shard, 'dp', axis=1, tiled=True)]
    pallas_call x1, Pallas kernels: 111 us -> 188 us  [local(): pl.pallas_call(pipeline_kernel, name='pipeline', out_shape=jax.ShapeDtype...]
  transfers between devices with their start and end apart: 2 -> 0, of which waited for: 2 -> 0; matrix products, arithmetic and copies ran while one was open for 0% -> 0% of each run, Pallas kernels for 0% -> 0%
where the time goes in v3:
time: 190 us; the launch traced here: 189 us
  Pallas kernels  188 us (99%)
    pallas_call x1, Pallas kernels, local(): pl.pallas_call(pipeline_kernel, name='pipeline', out_shape=jax.ShapeDtype...  188 us

profile of v3, /device:TPU:1, one launch (start us, length us, event | category | flops | bytes accessed | tf_op | source)
XLA Modules:
  0.0 189.2 jit_solution(10744632490203895085)
XLA Ops:
  0.0 187.7 %pipeline.1 = f32[16,1024]{1,0:T(8,128)} custom-call(bf16[192,1024]{1,0:T(8,128)(2,1)} %bitcast.5, bf16[192,1024]{1,0:T(8,128)(2,1)} %bitcast.6, s32[1,192]{1,0:T(1,128)} %seg_ref.1, bf16[3,16,1024]{2,1,0:T(8,128)(2,1)} %bitcast.8, bf16[16,1024]{1,0:T(8,128)(2,1)} %bitcast.9), custom_call_target="tpu_custom_call" | custom-call | tf_op jit(solution)/shard_map/pipeline/pallas_call | solution.py:370
  187.7 1.5 copy.7

commit v4 on v3

--- a/solution.py
+++ b/solution.py
@@ -11,6 +11,7 @@
 HEAD_DIM = 64
 PAIRS = HEADS // 2
 PAIR = 2 * HEAD_DIM
+WIDE = 128
 NC = 2
 SECTIONS = 8
 RING = 8
@@ -98,7 +99,7 @@
                         first(kind, way, wave + 1).start()
                     for onward in WAYS:
                         second(kind, -way * wave, onward, 1).start()
-        for a_index in range(RING):
+        for a_index in reversed(range(RING)):
             for kind in range(2):
                 a = offsets(kind)[a_index]
                 step = wave - abs(a)
@@ -133,11 +134,17 @@
     )
 
 
+def wide_halves(block, low):
+    zero = jnp.zeros_like(block)
+    gap = jnp.zeros((WIDE - block.shape[0], block.shape[1]), block.dtype)
+    return jnp.concatenate([jnp.where(low, block, zero), gap, jnp.where(low, zero, block), gap], axis=0)
+
+
 def pipeline_kernel(
     x_ref, cot_ref, seg_ref, attn_ref, out_ref, o_ref,
     w_ref, bias_ref, swap, gswap, mixes, gs, parts, ends,
     gsend1, grecv1, gsend2, grecv2, msend, mrecv, csend, crecv, esend, erecv, lsem,
-    hid, outb, gin, gout, qb, kb, vb, mixb, pb, dmb, dqb, dkb, dvb,
+    hid, outb, gin, gout, qb, kb, vb, mixb, pb, ptb, ktb, dsb, wtb, dmb, dqb, dkb, dvb,
     fsend, frecv, bsend, brecv,
 ):
     s = lax.axis_index("section")
@@ -182,8 +189,8 @@
         any_segment = lax.broadcast(lax.rem(s, 2), (length, length)) == 1
         allowed = (key <= query) & (same | any_segment)
         bias_ref[...] = jnp.where(allowed, 0.0, masked_score)
-        dkb[...] = jnp.zeros_like(dkb)
-        dvb[...] = jnp.zeros_like(dvb)
+        pb[...] = jnp.zeros_like(pb)
+        kb[length:] = jnp.zeros((kb.shape[0] - length, width), kb.dtype)
 
     def swap_rows(j):
         row = lax.broadcasted_iota(jnp.int32, (slice_cols, width), 0) + j * slice_cols
@@ -222,7 +229,17 @@
             device_id={"section": jnp.maximum(s - 1, 0)}, device_id_type=MESH,
         )
 
+    low_rows = lax.broadcasted_iota(jnp.int32, (PAIR, WIDE), 0) < HEAD_DIM
     low = lax.broadcasted_iota(jnp.int32, (rows_c, PAIR), 1) < HEAD_DIM
+
+    for j in range(4):
+        for i in range(RING):
+            block = w_ref[j, i].reshape(slice_cols, width)
+            wtb[j, :, i * slice_cols : (i + 1) * slice_cols] = block.T
+
+    @pl.when(s >= SECTIONS // 2)
+    def _():
+        gather_end(w_ref, gsend1, grecv1, gsend2, grecv2)
 
     for c in range(NC):
         lo, hi = c * rows_c, (c + 1) * rows_c
@@ -235,7 +252,7 @@
         r = lax.rsqrt(jnp.mean(h * h, axis=-1, keepdims=True) + epsilon)
         normed = (h * r).astype(jnp.bfloat16)
         for j, buf in ((0, qb), (1, kb), (2, vb)):
-            buf[lo:hi] = dot(normed, weight(j), NT).astype(jnp.bfloat16)
+            buf[lo:hi] = dot(normed, wtb[j], NN).astype(jnp.bfloat16)
         bias = bias_ref[lo:hi, :hi]
         bias2 = jnp.concatenate([bias, bias], axis=0)
         for p in range(PAIRS):
@@ -245,13 +262,16 @@
             top = jnp.max(scores, axis=-1, keepdims=True)
             e = jnp.exp(scores - top)
             weights = (e / jnp.sum(e, axis=-1, keepdims=True)).astype(jnp.bfloat16)
-            pb[c, p, :, :hi] = weights
-            o = dot(weights, vb[:hi, cols], NN)
-            mixb[lo:hi, cols] = jnp.where(low, o[:rows_c], o[rows_c:]).astype(jnp.bfloat16)
+            pb[c, p, :rows_c, :hi] = weights[:rows_c]
+            pb[c, p, WIDE : WIDE + rows_c, :hi] = weights[rows_c:]
+        for p in range(PAIRS):
+            cols = slice(p * PAIR, (p + 1) * PAIR)
+            o = dot(pb[c, p, :, :hi], vb[:hi, cols], NN)
+            mixb[lo:hi, cols] = jnp.where(low, o[:rows_c], o[WIDE : WIDE + rows_c]).astype(jnp.bfloat16)
 
         @pl.when(s < SECTIONS - 1)
         def _():
-            added = hid[lo:hi].astype(jnp.float32) + dot(mixb[lo:hi], weight(3), NT)
+            added = hid[lo:hi].astype(jnp.float32) + dot(mixb[lo:hi], wtb[3], NN)
             outb[lo:hi] = added.astype(jnp.bfloat16)
             forward_copy(c).start()
 
@@ -262,14 +282,32 @@
             mrecv.at[int(along_z)], along_z, k,
         )
 
-    def grad_copy(c, along_z, k):
-        rows = pl.ds(c * rows_c, rows_c)
+    def grad_copy(rows, c, along_z, k):
         source = gswap if along_z else gin
         return spread_copy(
             lambda there: source.at[rows, pl.ds(pl.multiple_of(there * slice_cols, slice_cols), slice_cols)],
             gs.at[int(along_z), k, rows], csend.at[int(along_z), c], crecv.at[int(along_z), c], along_z, k,
         )
 
+    def exchange(rows, c):
+        for k in ORDER:
+            grad_copy(rows, c, False, k).start()
+        gswap[rows] = dot(gin[rows], swap[...], NN).astype(jnp.bfloat16)
+        for k in ORDER:
+            grad_copy(rows, c, True, k).start()
+
+    def exchanged(along_z, act):
+        @pl.when(s == 0)
+        def _():
+            for k in ORDER:
+                for c in range(NC):
+                    act(grad_copy(pl.ds(c * rows_c, rows_c), c, along_z, k))
+
+        @pl.when(s > 0)
+        def _():
+            for k in ORDER:
+                act(grad_copy(pl.ds(0, length), 0, along_z, k))
+
     def end_copy(along_z, k):
         return spread_copy(
             lambda there: parts.at[int(not along_z), there], ends.at[int(not along_z), k - 1],
@@ -280,6 +318,26 @@
         for along_z in (False, True):
             mix_copy(along_z, k).start()
 
+    def mix_end():
+        for k in ORDER:
+            for along_z in (False, True):
+                mix_copy(along_z, k).wait_send()
+
+    @pl.when(s < SECTIONS // 2)
+    def _():
+        gather_end(w_ref, gsend1, grecv1, gsend2, grecv2)
+
+    @pl.when(s < 2)
+    def _():
+        mix_end()
+
+    for c in range(NC):
+        for p in range(PAIRS):
+            ptb[c, p] = pb[c, p].T
+    for p in range(PAIRS):
+        cols = slice(p * PAIR, (p + 1) * PAIR)
+        ktb[cols] = kb[:, cols].T
+
     for c in reversed(range(NC)):
         lo, hi = c * rows_c, (c + 1) * rows_c
 
@@ -293,18 +351,21 @@
             dmb[...] = dot(g, weight(3), NN).astype(jnp.bfloat16)
             for p in range(PAIRS):
                 cols = slice(p * PAIR, (p + 1) * PAIR)
-                d01 = halves(dmb[:, cols], low)
-                q01 = halves(qb[lo:hi, cols], low)
-                weights = pb[c, p, :, :hi]
-                wide = weights.astype(jnp.float32)
-                dweights = dot(d01, vb[:hi, cols], NT)
-                delta = jnp.sum(wide * dweights, axis=-1, keepdims=True)
-                ds = (wide * (dweights - delta) * HEAD_DIM ** (-0.5)).astype(jnp.bfloat16)
-                dq01 = dot(ds, kb[:hi, cols], NN)
-                dqb[:, cols] = jnp.where(low, dq01[:rows_c], dq01[rows_c:]).astype(jnp.bfloat16)
-                dkb[:hi, cols] += dot(ds, q01, TN)
-                dvb[:hi, cols] += dot(weights, d01, TN)
-            dn = dot(dqb[...], weight(0), NN)
+                d01 = wide_halves(dmb[:, cols], low)
+                turned = ptb[c, p, :hi]
+                wide = turned.astype(jnp.float32)
+                dweights = dot(vb[:hi, cols], d01, NT)
+                delta = jnp.sum(wide * dweights, axis=0, keepdims=True)
+                dsb[p, :hi] = (wide * (dweights - delta) * HEAD_DIM ** (-0.5)).astype(jnp.bfloat16)
+                dvalues = dot(turned, d01, NN)
+                dvb[:hi, cols] = dvalues if c == NC - 1 else dvb[:hi, cols] + dvalues
+            for p in range(PAIRS):
+                cols = slice(p * PAIR, (p + 1) * PAIR)
+                dq01 = dot(ktb[cols, :hi], dsb[p, :hi], NN)
+                dqb[cols] = jnp.where(low_rows, dq01[:, :WIDE], dq01[:, WIDE:]).astype(jnp.bfloat16)
+                dkeys = dot(dsb[p, :hi], wide_halves(qb[lo:hi, cols], low), NN)
+                dkb[:hi, cols] = dkeys if c == NC - 1 else dkb[:hi, cols] + dkeys
+            dn = dot(dqb[...], weight(0), TN)[:rows_c]
             dn += dot(dkb[lo:hi].astype(jnp.bfloat16), weight(1), NN)
             dn += dot(dvb[lo:hi].astype(jnp.bfloat16), weight(2), NN)
             h = hid[lo:hi].astype(jnp.float32)
@@ -314,11 +375,13 @@
             gout[lo:hi] = (g.astype(jnp.float32) + dh).astype(jnp.bfloat16)
             backward_copy(c).start()
 
-        for k in ORDER:
-            grad_copy(c, False, k).start()
-        gswap[lo:hi] = dot(gin[lo:hi], swap[...], NN).astype(jnp.bfloat16)
-        for k in ORDER:
-            grad_copy(c, True, k).start()
+        @pl.when(s == 0)
+        def _():
+            exchange(pl.ds(lo, rows_c), c)
+
+    @pl.when(s > 0)
+    def _():
+        exchange(pl.ds(0, length), 0)
 
     for along_z in (False, True):
         i, me, source = int(along_z), (z if along_z else y), (gswap if along_z else gin)
@@ -326,14 +389,20 @@
         gs[i, 0] = source[:, pl.ds(pl.multiple_of(me * slice_cols, slice_cols), slice_cols)]
         for k in ORDER:
             mix_copy(along_z, k).wait_recv()
-            for c in range(NC):
-                grad_copy(c, along_z, k).wait_recv()
+        exchanged(along_z, lambda copy: copy.wait_recv())
         total = dot(
             gs[i].reshape(RING * length, slice_cols), mixes[i].reshape(RING * length, half), TN
         )
         parts[i] = total.astype(jnp.bfloat16).reshape(RING, own, half)
         for k in ORDER:
             end_copy(not along_z, k).start()
+    for along_z in (False, True):
+        exchanged(along_z, lambda copy: copy.wait_send())
+
+    @pl.when(s >= 2)
+    def _():
+        mix_end()
+
     for along_z in (False, True):
         i, me = int(along_z), (y if along_z else z)
         total = parts[i, me].astype(jnp.float32)
@@ -344,11 +413,7 @@
 
     for along_z in (False, True):
         for k in ORDER:
-            mix_copy(along_z, k).wait_send()
             end_copy(along_z, k).wait_send()
-            for c in range(NC):
-                grad_copy(c, along_z, k).wait_send()
-    gather_end(w_ref, gsend1, grecv1, gsend2, grecv2)
     for c in range(NC):
         @pl.when(s < SECTIONS - 1)
         def _():
@@ -385,10 +450,14 @@
             dma(2, 2, 4), dma(2, 2, 4), dma(2, 9, 2, 4), dma(2, 9, 2, 4),
             dma(2, RING - 1), dma(2, RING - 1), dma(2, NC, RING - 1), dma(2, NC, RING - 1),
             dma(2, RING - 1), dma(2, RING - 1), dma(5),
-        ] + [full] * 8 + [
-            pltpu.VMEM((NC, PAIRS, 2 * rows_c, length), jnp.bfloat16),
+        ] + [full] * 5 + [pltpu.VMEM((2 * WIDE, width), jnp.bfloat16), full, full] + [
+            pltpu.VMEM((NC, PAIRS, 2 * WIDE, 2 * WIDE), jnp.bfloat16),
+            pltpu.VMEM((NC, PAIRS, 2 * WIDE, 2 * WIDE), jnp.bfloat16),
+            pltpu.VMEM((width, 2 * WIDE), jnp.bfloat16),
+            pltpu.VMEM((PAIRS, length, 2 * WIDE), jnp.bfloat16),
+            pltpu.VMEM((4, width, width), jnp.bfloat16),
             pltpu.VMEM((rows_c, width), jnp.bfloat16),
-            pltpu.VMEM((rows_c, width), jnp.bfloat16),
+            pltpu.VMEM((width, WIDE), jnp.bfloat16),
             pltpu.VMEM((length, width), jnp.float32),
             pltpu.VMEM((length, width), jnp.float32),
         ] + [dma(NC)] * 4,

time: 190 us -> 168 us (0.88)
  Pallas kernels: 188 us -> 166 us
    pallas_call x1, Pallas kernels: 188 us -> 166 us  [local(): pl.pallas_call(pipeline_kernel, name='pipeline', out_shape=jax.ShapeDtype...]
where the time goes in v4:
time: 168 us; the launch traced here: 167 us
  Pallas kernels  166 us (99%)
    pallas_call x1, Pallas kernels, local(): pl.pallas_call(pipeline_kernel, name='pipeline', out_shape=jax.ShapeDtype...  166 us

profile of v4, /device:TPU:1, one launch (start us, length us, event | category | flops | bytes accessed | tf_op | source)
XLA Modules:
  0.0 167.3 jit_solution(8532949433176446870)
XLA Ops:
  0.0 165.8 %pipeline.1 = f32[16,1024]{1,0:T(8,128)} custom-call(bf16[192,1024]{1,0:T(8,128)(2,1)} %bitcast.5, bf16[192,1024]{1,0:T(8,128)(2,1)} %bitcast.6, s32[1,192]{1,0:T(1,128)} %seg_ref.1, bf16[3,16,1024]{2,1,0:T(8,128)(2,1)} %bitcast.8, bf16[16,1024]{1,0:T(8,128)(2,1)} %bitcast.9), custom_call_target="tpu_custom_call" | custom-call | tf_op jit(solution)/shard_map/pipeline/pallas_call | solution.py:435
  165.8 1.5 copy.7

commit v5 on v4

--- a/solution.py
+++ b/solution.py
@@ -81,25 +81,38 @@
 WAYS = (1, -1)
 
 
-def gather(w_ref, send1, recv1, send2, recv2, beside):
+LIMIT = 6
+TURN = 2
+
+
+def gather(w_ref, send1, recv1, send2, recv2, beside, give_turn):
     first = functools.partial(first_copy, w_ref, send1, recv1)
     second = functools.partial(second_copy, w_ref, send2, recv2)
+    under_way = {(axis, way): [] for axis in range(2) for way in WAYS}
+
+    def start(axis, way, copy):
+        queue = under_way[axis, way]
+        if len(queue) == LIMIT:
+            queue.pop(0).wait_send()
+        copy.start()
+        queue.append(copy)
+
     for kind in range(2):
         for way in WAYS:
-            first(kind, way, 1).start()
+            start(kind, way, first(kind, way, 1))
     for kind in range(2):
         for way in WAYS:
-            second(kind, 0, way, 1).start()
+            start(1 - kind, way, second(kind, 0, way, 1))
     for wave in range(1, RING + 1):
         for kind in range(2):
             for way in WAYS:
                 if wave <= first_steps(kind, way):
                     first(kind, way, wave).wait_recv()
                     if wave < first_steps(kind, way):
-                        first(kind, way, wave + 1).start()
+                        start(kind, way, first(kind, way, wave + 1))
                     for onward in WAYS:
-                        second(kind, -way * wave, onward, 1).start()
-        for a_index in reversed(range(RING)):
+                        start(1 - kind, onward, second(kind, -way * wave, onward, 1))
+        for a_index in FAR:
             for kind in range(2):
                 a = offsets(kind)[a_index]
                 step = wave - abs(a)
@@ -107,18 +120,14 @@
                     if 1 <= step <= second_steps(a, way):
                         second(kind, a, way, step).wait_recv()
                         if step < second_steps(a, way):
-                            second(kind, a, way, step + 1).start()
+                            start(1 - kind, way, second(kind, a, way, step + 1))
         beside(wave)
-
-
-def gather_end(w_ref, send1, recv1, send2, recv2):
-    for kind in range(2):
-        for way in WAYS:
-            for step in range(1, first_steps(kind, way) + 1):
-                first_copy(w_ref, send1, recv1, kind, way, step).wait_send()
-            for a in offsets(kind):
-                for step in range(1, second_steps(a, way) + 1):
-                    second_copy(w_ref, send2, recv2, kind, a, way, step).wait_send()
+        if wave == TURN:
+            give_turn()
+    return [copy for queue in under_way.values() for copy in queue]
+
+
+FAR = tuple(reversed(range(RING)))
 
 
 ORDER = (4, 3, 5, 2, 6, 1, 7)
@@ -143,7 +152,7 @@
 def pipeline_kernel(
     x_ref, cot_ref, seg_ref, attn_ref, out_ref, o_ref,
     w_ref, bias_ref, swap, gswap, mixes, gs, parts, ends,
-    gsend1, grecv1, gsend2, grecv2, msend, mrecv, csend, crecv, esend, erecv, lsem,
+    gsend1, grecv1, gsend2, grecv2, msend, mrecv, csend, crecv, esend, erecv, lsem, turn,
     hid, outb, gin, gout, qb, kb, vb, mixb, pb, ptb, ktb, dsb, wtb, dmb, dqb, dkb, dvb,
     fsend, frecv, bsend, brecv,
 ):
@@ -203,7 +212,18 @@
         if wave == 4:
             mask()
 
-    gather(w_ref, gsend1, grecv1, gsend2, grecv2, beside)
+    lead = lax.rem(s, 2) == 0
+
+    def give_turn():
+        @pl.when(lead)
+        def _():
+            pl.semaphore_signal(turn, inc=1, device_id={"section": s + 1 - 2 * lax.rem(s, 2)}, device_id_type=MESH)
+
+    @pl.when(jnp.logical_not(lead))
+    def _():
+        pl.semaphore_wait(turn, 1)
+
+    unsent = gather(w_ref, gsend1, grecv1, gsend2, grecv2, beside, give_turn)
 
     @pl.when(s == 0)
     def _():
@@ -237,10 +257,6 @@
             block = w_ref[j, i].reshape(slice_cols, width)
             wtb[j, :, i * slice_cols : (i + 1) * slice_cols] = block.T
 
-    @pl.when(s >= SECTIONS // 2)
-    def _():
-        gather_end(w_ref, gsend1, grecv1, gsend2, grecv2)
-
     for c in range(NC):
         lo, hi = c * rows_c, (c + 1) * rows_c
 
@@ -251,19 +267,22 @@
         h = hid[lo:hi].astype(jnp.float32)
         r = lax.rsqrt(jnp.mean(h * h, axis=-1, keepdims=True) + epsilon)
         normed = (h * r).astype(jnp.bfloat16)
-        for j, buf in ((0, qb), (1, kb), (2, vb)):
-            buf[lo:hi] = dot(normed, wtb[j], NN).astype(jnp.bfloat16)
+        qb[lo:hi] = (dot(normed, wtb[0], NN) * HEAD_DIM ** (-0.5)).astype(jnp.bfloat16)
+        kb[lo:hi] = dot(normed, wtb[1], NN).astype(jnp.bfloat16)
         bias = bias_ref[lo:hi, :hi]
         bias2 = jnp.concatenate([bias, bias], axis=0)
         for p in range(PAIRS):
             cols = slice(p * PAIR, (p + 1) * PAIR)
             q01 = halves(qb[lo:hi, cols], low)
-            scores = dot(q01, kb[:hi, cols], NT) * HEAD_DIM ** (-0.5) + bias2
+            scores = dot(q01, kb[:hi, cols], NT) + bias2
             top = jnp.max(scores, axis=-1, keepdims=True)
             e = jnp.exp(scores - top)
-            weights = (e / jnp.sum(e, axis=-1, keepdims=True)).astype(jnp.bfloat16)
+            weights = (e * (1.0 / jnp.sum(e, axis=-1, keepdims=True))).astype(jnp.bfloat16)
             pb[c, p, :rows_c, :hi] = weights[:rows_c]
             pb[c, p, WIDE : WIDE + rows_c, :hi] = weights[rows_c:]
+            if p % 2 == 0:
+                two = slice(p * PAIR, (p + 2) * PAIR)
+                vb[lo:hi, two] = dot(normed, wtb[2, :, two], NN).astype(jnp.bfloat16)
         for p in range(PAIRS):
             cols = slice(p * PAIR, (p + 1) * PAIR)
             o = dot(pb[c, p, :, :hi], vb[:hi, cols], NN)
@@ -323,9 +342,8 @@
             for along_z in (False, True):
                 mix_copy(along_z, k).wait_send()
 
-    @pl.when(s < SECTIONS // 2)
-    def _():
-        gather_end(w_ref, gsend1, grecv1, gsend2, grecv2)
+    for copy in unsent:
+        copy.wait_send()
 
     @pl.when(s < 2)
     def _():
@@ -336,7 +354,7 @@
             ptb[c, p] = pb[c, p].T
     for p in range(PAIRS):
         cols = slice(p * PAIR, (p + 1) * PAIR)
-        ktb[cols] = kb[:, cols].T
+        ktb[cols] = (kb[:, cols] * HEAD_DIM ** (-0.5)).T
 
     for c in reversed(range(NC)):
         lo, hi = c * rows_c, (c + 1) * rows_c
@@ -356,7 +374,7 @@
                 wide = turned.astype(jnp.float32)
                 dweights = dot(vb[:hi, cols], d01, NT)
                 delta = jnp.sum(wide * dweights, axis=0, keepdims=True)
-                dsb[p, :hi] = (wide * (dweights - delta) * HEAD_DIM ** (-0.5)).astype(jnp.bfloat16)
+                dsb[p, :hi] = (wide * (dweights - delta)).astype(jnp.bfloat16)
                 dvalues = dot(turned, d01, NN)
                 dvb[:hi, cols] = dvalues if c == NC - 1 else dvb[:hi, cols] + dvalues
             for p in range(PAIRS):
@@ -449,7 +467,7 @@
             pltpu.VMEM((2, RING - 1, own, half), jnp.bfloat16),
             dma(2, 2, 4), dma(2, 2, 4), dma(2, 9, 2, 4), dma(2, 9, 2, 4),
             dma(2, RING - 1), dma(2, RING - 1), dma(2, NC, RING - 1), dma(2, NC, RING - 1),
-            dma(2, RING - 1), dma(2, RING - 1), dma(5),
+            dma(2, RING - 1), dma(2, RING - 1), dma(5), pltpu.SemaphoreType.REGULAR,
         ] + [full] * 5 + [pltpu.VMEM((2 * WIDE, width), jnp.bfloat16), full, full] + [
             pltpu.VMEM((NC, PAIRS, 2 * WIDE, 2 * WIDE), jnp.bfloat16),
             pltpu.VMEM((NC, PAIRS, 2 * WIDE, 2 * WIDE), jnp.bfloat16),

time: 168 us -> 164 us (0.976)
  Pallas kernels: 166 us -> 162 us
    pallas_call x1, Pallas kernels: 166 us -> 162 us  [local(): pl.pallas_call(pipeline_kernel, name='pipeline', out_shape=jax.ShapeDtype...]
where the time goes in v5:
time: 164 us; the launch traced here: 163 us
  Pallas kernels  162 us (99%)
    pallas_call x1, Pallas kernels, local(): pl.pallas_call(pipeline_kernel, name='pipeline', out_shape=jax.ShapeDtype...  162 us

profile of v5, /device:TPU:1, one launch (start us, length us, event | category | flops | bytes accessed | tf_op | source)
XLA Modules:
  0.0 163.3 jit_solution(14425047197053615271)
XLA Ops:
  0.0 161.8 %pipeline.1 = f32[16,1024]{1,0:T(8,128)} custom-call(bf16[192,1024]{1,0:T(8,128)(2,1)} %bitcast.5, bf16[192,1024]{1,0:T(8,128)(2,1)} %bitcast.6, s32[1,192]{1,0:T(1,128)} %seg_ref.1, bf16[3,16,1024]{2,1,0:T(8,128)(2,1)} %bitcast.8, bf16[16,1024]{1,0:T(8,128)(2,1)} %bitcast.9), custom_call_target="tpu_custom_call" | custom-call | tf_op jit(solution)/shard_map/pipeline/pallas_call | solution.py:453
  161.9 1.5 copy.7

commit v6 on v5

--- a/solution.py
+++ b/solution.py
@@ -13,6 +13,7 @@
 PAIR = 2 * HEAD_DIM
 WIDE = 128
 NC = 2
+BY_CHUNK = 2
 SECTIONS = 8
 RING = 8
 epsilon = 1e-05
@@ -249,6 +250,10 @@
             device_id={"section": jnp.maximum(s - 1, 0)}, device_id_type=MESH,
         )
 
+    def turn_weights(c):
+        for p in range(PAIRS):
+            ptb[c, p] = pb[c, p].T
+
     low_rows = lax.broadcasted_iota(jnp.int32, (PAIR, WIDE), 0) < HEAD_DIM
     low = lax.broadcasted_iota(jnp.int32, (rows_c, PAIR), 1) < HEAD_DIM
 
@@ -294,6 +299,11 @@
             outb[lo:hi] = added.astype(jnp.bfloat16)
             forward_copy(c).start()
 
+        if c == 0:
+            @pl.when(s == SECTIONS - 1)
+            def _():
+                turn_weights(0)
+
     def mix_copy(along_z, k):
         cols = pl.ds(half if along_z else 0, half)
         return spread_copy(
@@ -316,13 +326,13 @@
             grad_copy(rows, c, True, k).start()
 
     def exchanged(along_z, act):
-        @pl.when(s == 0)
+        @pl.when(s < BY_CHUNK)
         def _():
             for k in ORDER:
                 for c in range(NC):
                     act(grad_copy(pl.ds(c * rows_c, rows_c), c, along_z, k))
 
-        @pl.when(s > 0)
+        @pl.when(s >= BY_CHUNK)
         def _():
             for k in ORDER:
                 act(grad_copy(pl.ds(0, length), 0, along_z, k))
@@ -349,9 +359,12 @@
     def _():
         mix_end()
 
-    for c in range(NC):
-        for p in range(PAIRS):
-            ptb[c, p] = pb[c, p].T
+    @pl.when(s < SECTIONS - 1)
+    def _():
+        turn_weights(0)
+
+    for c in range(1, NC):
+        turn_weights(c)
     for p in range(PAIRS):
         cols = slice(p * PAIR, (p + 1) * PAIR)
         ktb[cols] = (kb[:, cols] * HEAD_DIM ** (-0.5)).T
@@ -393,11 +406,11 @@
             gout[lo:hi] = (g.astype(jnp.float32) + dh).astype(jnp.bfloat16)
             backward_copy(c).start()
 
-        @pl.when(s == 0)
+        @pl.when(s < BY_CHUNK)
         def _():
             exchange(pl.ds(lo, rows_c), c)
 
-    @pl.when(s > 0)
+    @pl.when(s >= BY_CHUNK)
     def _():
         exchange(pl.ds(0, length), 0)
 

time: 164 us -> 160 us (0.976)
  Pallas kernels: 162 us -> 159 us
    pallas_call x1, Pallas kernels: 162 us -> 159 us  [local(): pl.pallas_call(pipeline_kernel, name='pipeline', out_shape=jax.ShapeDtype...]
where the time goes in v6:
time: 160 us
  Pallas kernels  159 us (99%)
    pallas_call x1, Pallas kernels, local(): pl.pallas_call(pipeline_kernel, name='pipeline', out_shape=jax.ShapeDtype...  159 us

profile of v6, /device:TPU:1, one launch (start us, length us, event | category | flops | bytes accessed | tf_op | source)
XLA Modules:
  0.0 160.1 jit_solution(18107180641940374348)
XLA Ops:
  0.0 158.6 %pipeline.1 = f32[16,1024]{1,0:T(8,128)} custom-call(bf16[192,1024]{1,0:T(8,128)(2,1)} %bitcast.5, bf16[192,1024]{1,0:T(8,128)(2,1)} %bitcast.6, s32[1,192]{1,0:T(1,128)} %seg_ref.1, bf16[3,16,1024]{2,1,0:T(8,128)(2,1)} %bitcast.8, bf16[16,1024]{1,0:T(8,128)(2,1)} %bitcast.9), custom_call_target="tpu_custom_call" | custom-call | tf_op jit(solution)/shard_map/pipeline/pallas_call | solution.py:466
  158.6 1.5 copy.7

commit v7 on v6

--- a/solution.py
+++ b/solution.py
@@ -14,6 +14,7 @@
 WIDE = 128
 NC = 2
 BY_CHUNK = 2
+LATE = 6
 SECTIONS = 8
 RING = 8
 epsilon = 1e-05
@@ -250,6 +251,28 @@
             device_id={"section": jnp.maximum(s - 1, 0)}, device_id_type=MESH,
         )
 
+    def mix_copy(rows, c, along_z, k):
+        cols = pl.ds(half if along_z else 0, half)
+        return spread_copy(
+            lambda there: mixb.at[rows, cols], mixes.at[int(along_z), k, rows], msend.at[int(along_z), c],
+            mrecv.at[int(along_z), c], along_z, k,
+        )
+
+    def mix_each(rows, c, act):
+        for k in ORDER:
+            for along_z in (False, True):
+                act(mix_copy(rows, c, along_z, k))
+
+    def mix_all(act):
+        @pl.when(s < LATE)
+        def _():
+            mix_each(pl.ds(0, length), 0, act)
+
+        @pl.when(s >= LATE)
+        def _():
+            for c in range(NC):
+                mix_each(pl.ds(c * rows_c, rows_c), c, act)
+
     def turn_weights(c):
         for p in range(PAIRS):
             ptb[c, p] = pb[c, p].T
@@ -299,17 +322,14 @@
             outb[lo:hi] = added.astype(jnp.bfloat16)
             forward_copy(c).start()
 
+        @pl.when(s >= LATE)
+        def _():
+            mix_each(pl.ds(lo, rows_c), c, lambda copy: copy.start())
+
         if c == 0:
             @pl.when(s == SECTIONS - 1)
             def _():
                 turn_weights(0)
-
-    def mix_copy(along_z, k):
-        cols = pl.ds(half if along_z else 0, half)
-        return spread_copy(
-            lambda there: mixb.at[:, cols], mixes.at[int(along_z), k], msend.at[int(along_z)],
-            mrecv.at[int(along_z)], along_z, k,
-        )
 
     def grad_copy(rows, c, along_z, k):
         source = gswap if along_z else gin
@@ -343,21 +363,23 @@
             esend.at[int(not along_z)], erecv.at[int(not along_z)], along_z, k,
         )
 
-    for k in ORDER:
-        for along_z in (False, True):
-            mix_copy(along_z, k).start()
+    @pl.when(s < LATE)
+    def _():
+        mix_each(pl.ds(0, length), 0, lambda copy: copy.start())
 
     def mix_end():
-        for k in ORDER:
-            for along_z in (False, True):
-                mix_copy(along_z, k).wait_send()
+        mix_all(lambda copy: copy.wait_send())
 
     for copy in unsent:
         copy.wait_send()
 
+    def mix_received():
+        mix_all(lambda copy: copy.wait_recv())
+
     @pl.when(s < 2)
     def _():
         mix_end()
+        mix_received()
 
     @pl.when(s < SECTIONS - 1)
     def _():
@@ -414,12 +436,14 @@
     def _():
         exchange(pl.ds(0, length), 0)
 
+    @pl.when(s >= 2)
+    def _():
+        mix_received()
+
     for along_z in (False, True):
         i, me, source = int(along_z), (z if along_z else y), (gswap if along_z else gin)
         mixes[i, 0] = mixb[:, i * half : (i + 1) * half]
         gs[i, 0] = source[:, pl.ds(pl.multiple_of(me * slice_cols, slice_cols), slice_cols)]
-        for k in ORDER:
-            mix_copy(along_z, k).wait_recv()
         exchanged(along_z, lambda copy: copy.wait_recv())
         total = dot(
             gs[i].reshape(RING * length, slice_cols), mixes[i].reshape(RING * length, half), TN
@@ -479,7 +503,7 @@
             pltpu.VMEM((2, RING, own, half), jnp.bfloat16),
             pltpu.VMEM((2, RING - 1, own, half), jnp.bfloat16),
             dma(2, 2, 4), dma(2, 2, 4), dma(2, 9, 2, 4), dma(2, 9, 2, 4),
-            dma(2, RING - 1), dma(2, RING - 1), dma(2, NC, RING - 1), dma(2, NC, RING - 1),
+            dma(2, NC, RING - 1), dma(2, NC, RING - 1), dma(2, NC, RING - 1), dma(2, NC, RING - 1),
             dma(2, RING - 1), dma(2, RING - 1), dma(5), pltpu.SemaphoreType.REGULAR,
         ] + [full] * 5 + [pltpu.VMEM((2 * WIDE, width), jnp.bfloat16), full, full] + [
             pltpu.VMEM((NC, PAIRS, 2 * WIDE, 2 * WIDE), jnp.bfloat16),

time: 160 us -> 161 us (level)
  no operation moved by 1% of the time
where the time goes in v7:
time: 161 us; the launch traced here: 160 us
  Pallas kernels  159 us (99%)
    pallas_call x1, Pallas kernels, local(): pl.pallas_call(pipeline_kernel, name='pipeline', out_shape=jax.ShapeDtype...  159 us

profile of v7, /device:TPU:1, one launch (start us, length us, event | category | flops | bytes accessed | tf_op | source)
XLA Modules:
  0.0 160.2 jit_solution(9467489056936478439)
XLA Ops:
  0.0 158.7 %pipeline.1 = f32[16,1024]{1,0:T(8,128)} custom-call(bf16[192,1024]{1,0:T(8,128)(2,1)} %bitcast.5, bf16[192,1024]{1,0:T(8,128)(2,1)} %bitcast.6, s32[1,192]{1,0:T(1,128)} %seg_ref.1, bf16[3,16,1024]{2,1,0:T(8,128)(2,1)} %bitcast.8, bf16[16,1024]{1,0:T(8,128)(2,1)} %bitcast.9), custom_call_target="tpu_custom_call" | custom-call | tf_op jit(solution)/shard_map/pipeline/pallas_call | solution.py:490
  158.7 1.5 copy.7
